TPU v7x, 512 devices: a whole 4x4x16 slice. The times are simulated.
512 devices in a mesh: stream: 64 (over x, y, z_hi), trans: 8 (over z_lo, core).
Axes of the slice: x: 4, y: 4, z: 16 (z_hi: 4, z_lo: 4; z = z_hi * 4 + z_lo), core: 2. Of those that a mesh axis runs over, the one named last changes fastest.
Arguments:
- offsets: float32 [3, 8, 4096, 128], P(None, 'trans', 'stream'), may hold values from 0 to 1
- velocity: float32 [3, 8, 4096, 128], P(None, 'trans', 'stream'), may hold values from -6 to 6
- conc: float32 [4, 8, 4096, 128], P(None, 'trans', 'stream'), may hold values from 0.2 to 2
- potential: float32 [8, 4096, 128], P('trans', 'stream'), may hold values from -4 to 4
- mass: float32 [8, 4096, 128], P('trans', 'stream'), may hold values from 0.5 to 1.5
- density: float32 [8, 4096, 128], P('trans', 'stream'), may hold values from 0.7 to 1.4
- diffusivity: float32 [4], replicated, may hold values from 0.3 to 1.5
- valence: int32 [4], replicated, may hold values from -2 to 2
- pair_codes: int32 [8, 4096, 9], P('trans', 'stream'), may hold values from 0 to 15, as said below
Outputs:
- conc_new: float32 [4, 8, 4096, 128], P(None, 'trans', 'stream')
- velocity_new: float32 [3, 8, 4096, 128], P(None, 'trans', 'stream')
Inputs may be any that keep to these rules, and one draw needn't show every extreme that they name: `pair_codes`: an entry k below 15 names the tile k // 3 - 2 stream tiles downstream and k % 3 - 1 strips across, never outside the channel; the codes of one list are distinct and 7, the tile itself, is always listed; tiles of the first and the last strip list exactly 9 codes, all other tiles exactly 3 codes followed by 15s.
All inputs are finite; a program needn't handle non-finite values.
Results may differ from a plain program's by a relative error of at most 0.0003.
Values sent between devices are 32-bit elements; how exact they have to be, the bound alone decides.
No kernel may reach another device: no remote copies, remote signals or barrier semaphores. Data moves between devices by JAX's collectives and lax.ppermute only.
A program may use at most 64 MiB of HBM per device.

v0:
```python
from functools import partial

import jax
import jax.numpy as jnp
from jax import lax
from jax.sharding import PartitionSpec as P

support = 2.5
weight_scale = 1.0 / 128.0
time_step = 0.1
viscosity = 0.5
empty_code = 15
highest = lax.Precision.HIGHEST
pair_limit = 72


def padded(cells, sides, width):
    for axis, dim in sides:
        count = lax.axis_size(axis)
        head = lax.slice_in_dim(cells, 0, width, axis=dim)
        tail = lax.slice_in_dim(cells, cells.shape[dim] - width, cells.shape[dim], axis=dim)
        cells = jnp.concatenate(
            [
                lax.ppermute(tail, axis, [(i, (i + 1) % count) for i in range(count)]),
                cells,
                lax.ppermute(head, axis, [((i + 1) % count, i) for i in range(count)]),
            ],
            axis=dim,
        )
    return cells


def kernel_matrix(own_pos, near_pos, near_vol, shift, weight):
    delta = own_pos[:, :, None] - near_pos[:, None, :] - shift[:, None, None]
    radius = jnp.sqrt(jnp.sum(delta * delta, axis=0))
    base = jnp.maximum(1.0 - radius / support, 0.0)
    return weight * weight_scale * (base * base * base) * near_vol[None, :]


def flux_pair(own, near, shift, weight, charge_num):
    link = kernel_matrix(own[0:3], near[0:3], near[3], shift, weight)
    conc_near = near[4:8]
    phi_near = near[8]
    ones = jnp.ones_like(phi_near)
    rows = jnp.concatenate(
        [
            ones[None],
            conc_near,
            phi_near[None],
            conc_near * phi_near[None],
            near[0:3],
            phi_near[None] * near[0:3],
        ],
        axis=0,
    )
    moment = jnp.dot(rows, link.T, precision=highest, preferred_element_type=jnp.float32)
    total = moment[0]
    link_conc = moment[1:5]
    link_phi = moment[5]
    link_cphi = moment[6:10]
    link_pos = moment[10:13]
    link_ppos = moment[13:16]
    conc_own = own[4:8]
    phi_own = own[8]
    spread_phi = link_phi - phi_own * total
    flux = 2.0 * (link_conc - conc_own * total) + charge_num[:, None] * (
        conc_own * spread_phi + link_cphi - phi_own * link_conc
    )
    rel = own[0:3] - shift[:, None]
    grad = rel * spread_phi - (link_ppos - phi_own * link_pos)
    return jnp.concatenate([flux, grad], axis=0)


def force_pair(own, near, shift, weight):
    link = kernel_matrix(own[0:3], near[0:3], near[3], shift, weight)
    press_near = near[4]
    pos_near = near[0:3]
    ones = jnp.ones_like(press_near)
    rows = jnp.concatenate(
        [ones[None], pos_near, press_near[None], press_near[None] * pos_near, near[5:8]], axis=0
    )
    moment = jnp.dot(rows, link.T, precision=highest, preferred_element_type=jnp.float32)
    total = moment[0]
    link_pos = moment[1:4]
    link_press = moment[4]
    link_ppos = moment[5:8]
    link_vel = moment[8:11]
    rel = own[0:3] - shift[:, None]
    press_own = own[4]
    push = press_own * (total * rel - link_pos) + rel * link_press - link_ppos
    drag = link_vel - own[5:8] * total
    return jnp.concatenate([push, drag], axis=0)


def pair_sum(pair_fn, own, near, codes):
    live = codes < empty_code
    safe = jnp.where(live, codes, 7)
    shift = jnp.stack([safe // 3 - 2, safe % 3 - 1, jnp.zeros_like(safe)], axis=-1).astype(
        jnp.float32
    )
    weight = live.astype(jnp.float32)
    inner = jax.vmap(pair_fn, in_axes=(None, 1, 0, 0))
    outer = jax.vmap(inner, in_axes=(1, 1, 0, 0))
    return jnp.sum(outer(own, near, shift, weight), axis=1)


def block_tiles(count, pairs_each):
    limit = max(1, pair_limit // pairs_each)
    size = 1
    while size * 2 <= limit and count % (size * 2) == 0:
        size = size * 2
    return size


def owner_sums(extended, codes, pair_fn):
    rows, height, span, width = extended.shape
    count = span - 4
    flat = extended.reshape(rows, height * span, width)
    listed = codes.reshape(count, codes.shape[-1])
    live = listed < empty_code
    safe = jnp.where(live, listed, 7)
    start = jnp.arange(count, dtype=jnp.int32)
    index = safe % 3 * span + start[:, None] + safe // 3
    home = span + start + 2
    step_tiles = block_tiles(count, listed.shape[1])

    def one_group(group):
        first = group * step_tiles
        own = jnp.take(flat, lax.dynamic_slice_in_dim(home, first, step_tiles, 0), axis=1)
        near = jnp.take(flat, lax.dynamic_slice_in_dim(index, first, step_tiles, 0), axis=1)
        return pair_sum(pair_fn, own, near, lax.dynamic_slice_in_dim(listed, first, step_tiles, 0))

    result = lax.map(one_group, jnp.arange(count // step_tiles, dtype=jnp.int32))
    result = result.reshape(count, result.shape[2], width)
    return jnp.transpose(result, (1, 0, 2))[:, None]


def per_device(offsets, velocity, conc, potential, mass, density, diffusivity, valence, pair_codes):
    charge_num = valence.astype(jnp.float32)
    vol = mass / density
    first = jnp.concatenate([offsets, vol[None], conc, potential[None]], axis=0)
    flux_fn = partial(flux_pair, charge_num=charge_num)
    widened = padded(first, (("stream", 2),), 2)
    extended = padded(widened, (("trans", 1),), 1)
    sums_one = owner_sums(extended, pair_codes, flux_fn)
    conc_new = conc + time_step * diffusivity[:, None, None, None] * sums_one[0:4]
    field = sums_one[4:7] + jnp.array([1.0, 0.0, 0.0], dtype=jnp.float32)[:, None, None, None]
    charge = jnp.sum(charge_num[:, None, None, None] * conc_new, axis=0)
    vstar = velocity + time_step * charge[None] * field / density[None]
    press = jnp.sum(conc_new, axis=0)
    second = jnp.concatenate([press[None], vstar], axis=0)
    widened_two = padded(second, (("stream", 2),), 2)
    outer_two = padded(widened_two, (("trans", 1),), 1)
    sums_two = owner_sums(
        jnp.concatenate([extended[0:4], outer_two], axis=0), pair_codes, force_pair
    )
    accel = sums_two[0:3] / density[None] + 2.0 * viscosity * sums_two[3:6]
    velocity_new = vstar + time_step * accel
    return (conc_new, velocity_new)


def solution(mesh):
    placed = (
        P(None, "trans", "stream", None),
        P(None, "trans", "stream", None),
        P(None, "trans", "stream", None),
        P("trans", "stream", None),
        P("trans", "stream", None),
        P("trans", "stream", None),
        P(),
        P(),
        P("trans", "stream", None),
    )
    return jax.shard_map(
        per_device,
        mesh=mesh,
        in_specs=placed,
        out_specs=(P(None, "trans", "stream", None), P(None, "trans", "stream", None)),
        check_vma=False,
    )
```

profile of v0, /device:TPU:1, one launch (start us, length us, event | category | flops | bytes accessed | tf_op | source)
XLA Modules:
  0.0 367.7 jit_solution(16820425001221314316)
XLA Ops:
  0.6 1.0 copy.130
  1.6 1.0 copy.122
  2.6 0.8 div.56
  3.4 0.7 pad_maximum_fusion.6
  4.1 17.9 %collective-permute-start.1 = (f32[9,1,2,128]{3,0,2,1:T(8,128)S(1)}, f32[9,1,2,128]{3,0,2,1:T(8,128)S(1)}, u32[]{:S(2)}, u32[]{:S(2)}) collective-permute-start(f32[9,1,2,128]{3,0,2,1:T(8,128)S(1)} %get-tuple-element.358), channel_id=1, source_target_pairs={{8,0},{16,8},{24,16},{32,24},{40,32},{48,40},{56,48},{64,56},{72,6... | collective-permute-start | bytes 27656 | tf_op jit(solution)/shard_map/ppermute | solution.py:26
  22.0 1.9 collective-permute-start
  25.3 0.8 copy.121
  26.1 8.7 %collective-permute-done = f32[9,1,2,128]{3,0,2,1:T(8,128)S(1)} collective-permute-done((f32[9,1,2,128]{3,0,2,1:T(8,128)S(1)}, f32[9,1,2,128]{3,0,2,1:T(8,128)S(1)}, u32[]{:S(2)}, u32[]{:S(2)}) %collective-permute-start) | collective-permute-done | bytes 9248 | tf_op jit(solution)/shard_map/ppermute | solution.py:24
  34.7 0.9 pad_maximum_fusion.1
  36.0 3.9 %collective-permute-start.3 = (f32[9,1,68,128]{3,1,2,0:T(1,128)S(1)}, f32[9,1,68,128]{3,1,2,0:T(1,128)S(1)}, u32[]{:S(2)}, u32[]{:S(2)}) collective-permute-start(f32[9,1,68,128]{3,1,2,0:T(1,128)S(1)} %copy.124), channel_id=1, source_target_pairs={{1,0},{2,1},{3,2},{4,3},{5,4},{6,5},{7,6},{0,7},{9,8},{10,9},{11,1... | collective-permute-start | bytes 940040 | tf_op jit(solution)/shard_map/ppermute | solution.py:26
  39.9 2.5 collective-permute-start.2
  42.5 2.6 collective-permute-done.3
  45.2 2.1 collective-permute-done.2
  47.4 1.0 pad_maximum_fusion
  48.4 153.3 %while.26 = (s32[]{:T(128)}, f32[8,8,7,128]{3,2,1,0:T(8,128)S(1)}, s32[8]{0:T(128)S(1)}, s32[64,9]{1,0:T(8,128)S(1)}, f32[9,204,128]{2,0,1:T(8,128)S(1)}, /*inde...) while((s32[]{:T(128)}, f32[8,8,7,128]{3,2,1,0:T(8,128)S(1)}, ...), condition=%wide.region_3.4_spmd, body=%wide.region_0.3_spmd.sunk | while | flops 248497536 | bytes 16560839 | solution.py:133
  50.9 2.0 concatenate.88
  53.9 4.4 %multiply_reduce_fusion.5 = f32[8,9,128,128]{3,2,1,0:T(8,128)S(1)} fusion(f32[8,9,3]{2,1,0:T(8,128)S(1)} %copy.169, f32[8,9,3,128]{3,2,1,0:T(4,128)S(1)} %slice_bitcast_fusion.17, f32[8,3,128]{2,1,0:T(4,128)S(1)} %slice_bitcast_fusion.18), kind=kLoop, calls=%fused_computation.4.clone.1 | loop fusion | flops 12976128 | bytes 4842336 | tf_op jit(solution)/shard_map/while/body/eval_jaxpr/vmap(vmap())/reduce_sum | solution.py:35
  58.4 8.6 %fusion.88 = f32[8,9,16,128]{3,2,1,0:T(8,128)S(1)} fusion(f32[8,9,16,128]{3,2,1,0:T(8,128)S(1)} %concatenate.88, f32[8,9,128,128]{3,2,1,0:T(8,128)S(1)} %multiply_reduce_fusion.5, f32[8,9,128]{2,1,0:T(8,128)S(1)} %get-tuple-element.488, f32[8,9]{1,0:T(8,128)S(1)} %compare_select_fusion.15), kind=kOutput, calls=%fused_computation.8.clone.1 | convolution fusion | flops 234749952 | bytes 5935392 | tf_op jit(solution)/shard_map/while/body/eval_jaxpr/vmap(vmap())/dot_general | solution.py:56
  70.0 2.0 concatenate.88
  73.1 4.4 %multiply_reduce_fusion.5 = f32[8,9,128,128]{3,2,1,0:T(8,128)S(1)} fusion(f32[8,9,3]{2,1,0:T(8,128)S(1)} %copy.169, f32[8,9,3,128]{3,2,1,0:T(4,128)S(1)} %slice_bitcast_fusion.17, f32[8,3,128]{2,1,0:T(4,128)S(1)} %slice_bitcast_fusion.18), kind=kLoop, calls=%fused_computation.4.clone.1 | loop fusion | flops 12976128 | bytes 4842336 | tf_op jit(solution)/shard_map/while/body/eval_jaxpr/vmap(vmap())/reduce_sum | solution.py:35
  77.5 8.6 %fusion.88 = f32[8,9,16,128]{3,2,1,0:T(8,128)S(1)} fusion(f32[8,9,16,128]{3,2,1,0:T(8,128)S(1)} %concatenate.88, f32[8,9,128,128]{3,2,1,0:T(8,128)S(1)} %multiply_reduce_fusion.5, f32[8,9,128]{2,1,0:T(8,128)S(1)} %get-tuple-element.488, f32[8,9]{1,0:T(8,128)S(1)} %compare_select_fusion.15), kind=kOutput, calls=%fused_computation.8.clone.1 | convolution fusion | flops 234749952 | bytes 5935392 | tf_op jit(solution)/shard_map/while/body/eval_jaxpr/vmap(vmap())/dot_general | solution.py:56
  89.2 2.0 concatenate.88
  92.3 4.4 %multiply_reduce_fusion.5 = f32[8,9,128,128]{3,2,1,0:T(8,128)S(1)} fusion(f32[8,9,3]{2,1,0:T(8,128)S(1)} %copy.169, f32[8,9,3,128]{3,2,1,0:T(4,128)S(1)} %slice_bitcast_fusion.17, f32[8,3,128]{2,1,0:T(4,128)S(1)} %slice_bitcast_fusion.18), kind=kLoop, calls=%fused_computation.4.clone.1 | loop fusion | flops 12976128 | bytes 4842336 | tf_op jit(solution)/shard_map/while/body/eval_jaxpr/vmap(vmap())/reduce_sum | solution.py:35
  96.7 8.6 %fusion.88 = f32[8,9,16,128]{3,2,1,0:T(8,128)S(1)} fusion(f32[8,9,16,128]{3,2,1,0:T(8,128)S(1)} %concatenate.88, f32[8,9,128,128]{3,2,1,0:T(8,128)S(1)} %multiply_reduce_fusion.5, f32[8,9,128]{2,1,0:T(8,128)S(1)} %get-tuple-element.488, f32[8,9]{1,0:T(8,128)S(1)} %compare_select_fusion.15), kind=kOutput, calls=%fused_computation.8.clone.1 | convolution fusion | flops 234749952 | bytes 5935392 | tf_op jit(solution)/shard_map/while/body/eval_jaxpr/vmap(vmap())/dot_general | solution.py:56
  108.3 2.0 concatenate.88
  111.4 4.4 %multiply_reduce_fusion.5 = f32[8,9,128,128]{3,2,1,0:T(8,128)S(1)} fusion(f32[8,9,3]{2,1,0:T(8,128)S(1)} %copy.169, f32[8,9,3,128]{3,2,1,0:T(4,128)S(1)} %slice_bitcast_fusion.17, f32[8,3,128]{2,1,0:T(4,128)S(1)} %slice_bitcast_fusion.18), kind=kLoop, calls=%fused_computation.4.clone.1 | loop fusion | flops 12976128 | bytes 4842336 | tf_op jit(solution)/shard_map/while/body/eval_jaxpr/vmap(vmap())/reduce_sum | solution.py:35
  115.8 8.6 %fusion.88 = f32[8,9,16,128]{3,2,1,0:T(8,128)S(1)} fusion(f32[8,9,16,128]{3,2,1,0:T(8,128)S(1)} %concatenate.88, f32[8,9,128,128]{3,2,1,0:T(8,128)S(1)} %multiply_reduce_fusion.5, f32[8,9,128]{2,1,0:T(8,128)S(1)} %get-tuple-element.488, f32[8,9]{1,0:T(8,128)S(1)} %compare_select_fusion.15), kind=kOutput, calls=%fused_computation.8.clone.1 | convolution fusion | flops 234749952 | bytes 5935392 | tf_op jit(solution)/shard_map/while/body/eval_jaxpr/vmap(vmap())/dot_general | solution.py:56
  127.5 2.0 concatenate.88
  130.6 4.4 %multiply_reduce_fusion.5 = f32[8,9,128,128]{3,2,1,0:T(8,128)S(1)} fusion(f32[8,9,3]{2,1,0:T(8,128)S(1)} %copy.169, f32[8,9,3,128]{3,2,1,0:T(4,128)S(1)} %slice_bitcast_fusion.17, f32[8,3,128]{2,1,0:T(4,128)S(1)} %slice_bitcast_fusion.18), kind=kLoop, calls=%fused_computation.4.clone.1 | loop fusion | flops 12976128 | bytes 4842336 | tf_op jit(solution)/shard_map/while/body/eval_jaxpr/vmap(vmap())/reduce_sum | solution.py:35
  135.0 8.6 %fusion.88 = f32[8,9,16,128]{3,2,1,0:T(8,128)S(1)} fusion(f32[8,9,16,128]{3,2,1,0:T(8,128)S(1)} %concatenate.88, f32[8,9,128,128]{3,2,1,0:T(8,128)S(1)} %multiply_reduce_fusion.5, f32[8,9,128]{2,1,0:T(8,128)S(1)} %get-tuple-element.488, f32[8,9]{1,0:T(8,128)S(1)} %compare_select_fusion.15), kind=kOutput, calls=%fused_computation.8.clone.1 | convolution fusion | flops 234749952 | bytes 5935392 | tf_op jit(solution)/shard_map/while/body/eval_jaxpr/vmap(vmap())/dot_general | solution.py:56
  146.7 2.0 concatenate.88
  149.7 4.4 %multiply_reduce_fusion.5 = f32[8,9,128,128]{3,2,1,0:T(8,128)S(1)} fusion(f32[8,9,3]{2,1,0:T(8,128)S(1)} %copy.169, f32[8,9,3,128]{3,2,1,0:T(4,128)S(1)} %slice_bitcast_fusion.17, f32[8,3,128]{2,1,0:T(4,128)S(1)} %slice_bitcast_fusion.18), kind=kLoop, calls=%fused_computation.4.clone.1 | loop fusion | flops 12976128 | bytes 4842336 | tf_op jit(solution)/shard_map/while/body/eval_jaxpr/vmap(vmap())/reduce_sum | solution.py:35
  154.2 8.6 %fusion.88 = f32[8,9,16,128]{3,2,1,0:T(8,128)S(1)} fusion(f32[8,9,16,128]{3,2,1,0:T(8,128)S(1)} %concatenate.88, f32[8,9,128,128]{3,2,1,0:T(8,128)S(1)} %multiply_reduce_fusion.5, f32[8,9,128]{2,1,0:T(8,128)S(1)} %get-tuple-element.488, f32[8,9]{1,0:T(8,128)S(1)} %compare_select_fusion.15), kind=kOutput, calls=%fused_computation.8.clone.1 | convolution fusion | flops 234749952 | bytes 5935392 | tf_op jit(solution)/shard_map/while/body/eval_jaxpr/vmap(vmap())/dot_general | solution.py:56
  165.8 2.0 concatenate.88
  168.9 4.4 %multiply_reduce_fusion.5 = f32[8,9,128,128]{3,2,1,0:T(8,128)S(1)} fusion(f32[8,9,3]{2,1,0:T(8,128)S(1)} %copy.169, f32[8,9,3,128]{3,2,1,0:T(4,128)S(1)} %slice_bitcast_fusion.17, f32[8,3,128]{2,1,0:T(4,128)S(1)} %slice_bitcast_fusion.18), kind=kLoop, calls=%fused_computation.4.clone.1 | loop fusion | flops 12976128 | bytes 4842336 | tf_op jit(solution)/shard_map/while/body/eval_jaxpr/vmap(vmap())/reduce_sum | solution.py:35
  173.3 8.6 %fusion.88 = f32[8,9,16,128]{3,2,1,0:T(8,128)S(1)} fusion(f32[8,9,16,128]{3,2,1,0:T(8,128)S(1)} %concatenate.88, f32[8,9,128,128]{3,2,1,0:T(8,128)S(1)} %multiply_reduce_fusion.5, f32[8,9,128]{2,1,0:T(8,128)S(1)} %get-tuple-element.488, f32[8,9]{1,0:T(8,128)S(1)} %compare_select_fusion.15), kind=kOutput, calls=%fused_computation.8.clone.1 | convolution fusion | flops 234749952 | bytes 5935392 | tf_op jit(solution)/shard_map/while/body/eval_jaxpr/vmap(vmap())/dot_general | solution.py:56
  185.0 2.0 concatenate.88
  188.0 4.4 %multiply_reduce_fusion.5 = f32[8,9,128,128]{3,2,1,0:T(8,128)S(1)} fusion(f32[8,9,3]{2,1,0:T(8,128)S(1)} %copy.169, f32[8,9,3,128]{3,2,1,0:T(4,128)S(1)} %slice_bitcast_fusion.17, f32[8,3,128]{2,1,0:T(4,128)S(1)} %slice_bitcast_fusion.18), kind=kLoop, calls=%fused_computation.4.clone.1 | loop fusion | flops 12976128 | bytes 4842336 | tf_op jit(solution)/shard_map/while/body/eval_jaxpr/vmap(vmap())/reduce_sum | solution.py:35
  192.5 8.6 %fusion.88 = f32[8,9,16,128]{3,2,1,0:T(8,128)S(1)} fusion(f32[8,9,16,128]{3,2,1,0:T(8,128)S(1)} %concatenate.88, f32[8,9,128,128]{3,2,1,0:T(8,128)S(1)} %multiply_reduce_fusion.5, f32[8,9,128]{2,1,0:T(8,128)S(1)} %get-tuple-element.488, f32[8,9]{1,0:T(8,128)S(1)} %compare_select_fusion.15), kind=kOutput, calls=%fused_computation.8.clone.1 | convolution fusion | flops 234749952 | bytes 5935392 | tf_op jit(solution)/shard_map/while/body/eval_jaxpr/vmap(vmap())/dot_general | solution.py:56
  202.0 1.0 fusion.54
  203.1 2.8 collective-permute-start.5
  205.9 6.5 %collective-permute-start.4 = (f32[4,1,2,128]{3,0,2,1:T(4,128)S(1)}, f32[4,1,2,128]{3,0,2,1:T(4,128)S(1)}, u32[]{:S(2)}, u32[]{:S(2)}) collective-permute-start(f32[4,1,2,128]{3,0,2,1:T(4,128)S(1)} %get-tuple-element.359), channel_id=1, source_target_pairs={{0,8},{8,16},{16,24},{24,32},{32,40},{40,48},{48,56},{56,64},{64,7... | collective-permute-start | bytes 12296 | tf_op jit(solution)/shard_map/ppermute | solution.py:24
  212.5 5.9 %collective-permute-done.4 = f32[4,1,2,128]{3,0,2,1:T(4,128)S(1)} collective-permute-done((f32[4,1,2,128]{3,0,2,1:T(4,128)S(1)}, f32[4,1,2,128]{3,0,2,1:T(4,128)S(1)}, u32[]{:S(2)}, u32[]{:S(2)}) %collective-permute-start.4) | collective-permute-done | bytes 4128 | tf_op jit(solution)/shard_map/ppermute | solution.py:24
  218.5 6.0 %collective-permute-start.7 = (f32[4,1,68,128]{3,0,2,1:T(4,128)S(1)}, f32[4,1,68,128]{3,0,2,1:T(4,128)S(1)}, u32[]{:S(2)}, u32[]{:S(2)}) collective-permute-start(f32[4,1,68,128]{3,0,2,1:T(4,128)S(1)} %pad_maximum_fusion.2), channel_id=1, source_target_pairs={{1,0},{2,1},{3,2},{4,3},{5,4},{6,5},{7,6},{0,7},{9,8},{10,9},{11,1... | collective-permute-start | bytes 417800 | tf_op jit(solution)/shard_map/ppermute | solution.py:26
  224.5 1.9 collective-permute-start.6
  226.5 0.7 copy.132
  227.1 1.3 collective-permute-done.6
  228.6 138.3 %while.27 = (s32[]{:T(128)}, f32[8,8,6,128]{3,2,1,0:T(8,128)S(1)}, s32[8]{0:T(128)S(1)}, s32[64]{0:T(128)S(1)}, f32[8,204,128]{2,0,1:T(8,128)S(1)}, /*index=5*/s...) while((s32[]{:T(128)}, f32[8,8,6,128]{3,2,1,0:T(8,128)S(1)}, ...), condition=%wide.region_9.10_spmd, body=%wide.region_6.9_spmd.sunk | while | flops 177414528 | bytes 14934703 | solution.py:133
  232.4 4.4 %multiply_reduce_fusion.6 = f32[8,9,128,128]{3,2,1,0:T(8,128)S(1)} fusion(f32[8,9,3]{2,1,0:T(8,128)S(1)} %copy.173, f32[8,9,3,128]{3,2,1,0:T(4,128)S(1)} %get-tuple-element.500, f32[8,3,128]{2,1,0:T(4,128)S(1)} %get-tuple-element.510), kind=kLoop, calls=%fused_computation.62.clone.1 | loop fusion | flops 12976128 | bytes 4842336 | tf_op jit(solution)/shard_map/while/body/eval_jaxpr/vmap(vmap())/reduce_sum | solution.py:35
  236.9 8.6 %fusion.96 = f32[8,9,11,128]{3,2,1,0:T(8,128)S(1)} fusion(f32[8,9,11,128]{3,2,1,0:T(8,128)S(1)} %concatenate.89, f32[8,9,128,128]{3,2,1,0:T(8,128)S(1)} %multiply_reduce_fusion.6, f32[8,9,128]{2,1,0:T(8,128)S(1)} %get-tuple-element.511, f32[8,9]{1,0:T(8,128)S(1)} %compare_select_fusion.16), kind=kOutput, calls=%fused_computation.66.clone.1 | convolution fusion | flops 163971072 | bytes 5566752 | tf_op jit(solution)/shard_map/while/body/eval_jaxpr/vmap(vmap())/dot_general | solution.py:82
  249.7 4.4 %multiply_reduce_fusion.6 = f32[8,9,128,128]{3,2,1,0:T(8,128)S(1)} fusion(f32[8,9,3]{2,1,0:T(8,128)S(1)} %copy.173, f32[8,9,3,128]{3,2,1,0:T(4,128)S(1)} %get-tuple-element.500, f32[8,3,128]{2,1,0:T(4,128)S(1)} %get-tuple-element.510), kind=kLoop, calls=%fused_computation.62.clone.1 | loop fusion | flops 12976128 | bytes 4842336 | tf_op jit(solution)/shard_map/while/body/eval_jaxpr/vmap(vmap())/reduce_sum | solution.py:35
  254.1 8.6 %fusion.96 = f32[8,9,11,128]{3,2,1,0:T(8,128)S(1)} fusion(f32[8,9,11,128]{3,2,1,0:T(8,128)S(1)} %concatenate.89, f32[8,9,128,128]{3,2,1,0:T(8,128)S(1)} %multiply_reduce_fusion.6, f32[8,9,128]{2,1,0:T(8,128)S(1)} %get-tuple-element.511, f32[8,9]{1,0:T(8,128)S(1)} %compare_select_fusion.16), kind=kOutput, calls=%fused_computation.66.clone.1 | convolution fusion | flops 163971072 | bytes 5566752 | tf_op jit(solution)/shard_map/while/body/eval_jaxpr/vmap(vmap())/dot_general | solution.py:82
  267.0 4.4 %multiply_reduce_fusion.6 = f32[8,9,128,128]{3,2,1,0:T(8,128)S(1)} fusion(f32[8,9,3]{2,1,0:T(8,128)S(1)} %copy.173, f32[8,9,3,128]{3,2,1,0:T(4,128)S(1)} %get-tuple-element.500, f32[8,3,128]{2,1,0:T(4,128)S(1)} %get-tuple-element.510), kind=kLoop, calls=%fused_computation.62.clone.1 | loop fusion | flops 12976128 | bytes 4842336 | tf_op jit(solution)/shard_map/while/body/eval_jaxpr/vmap(vmap())/reduce_sum | solution.py:35
  271.4 8.6 %fusion.96 = f32[8,9,11,128]{3,2,1,0:T(8,128)S(1)} fusion(f32[8,9,11,128]{3,2,1,0:T(8,128)S(1)} %concatenate.89, f32[8,9,128,128]{3,2,1,0:T(8,128)S(1)} %multiply_reduce_fusion.6, f32[8,9,128]{2,1,0:T(8,128)S(1)} %get-tuple-element.511, f32[8,9]{1,0:T(8,128)S(1)} %compare_select_fusion.16), kind=kOutput, calls=%fused_computation.66.clone.1 | convolution fusion | flops 163971072 | bytes 5566752 | tf_op jit(solution)/shard_map/while/body/eval_jaxpr/vmap(vmap())/dot_general | solution.py:82
  284.3 4.4 %multiply_reduce_fusion.6 = f32[8,9,128,128]{3,2,1,0:T(8,128)S(1)} fusion(f32[8,9,3]{2,1,0:T(8,128)S(1)} %copy.173, f32[8,9,3,128]{3,2,1,0:T(4,128)S(1)} %get-tuple-element.500, f32[8,3,128]{2,1,0:T(4,128)S(1)} %get-tuple-element.510), kind=kLoop, calls=%fused_computation.62.clone.1 | loop fusion | flops 12976128 | bytes 4842336 | tf_op jit(solution)/shard_map/while/body/eval_jaxpr/vmap(vmap())/reduce_sum | solution.py:35
  288.7 8.6 %fusion.96 = f32[8,9,11,128]{3,2,1,0:T(8,128)S(1)} fusion(f32[8,9,11,128]{3,2,1,0:T(8,128)S(1)} %concatenate.89, f32[8,9,128,128]{3,2,1,0:T(8,128)S(1)} %multiply_reduce_fusion.6, f32[8,9,128]{2,1,0:T(8,128)S(1)} %get-tuple-element.511, f32[8,9]{1,0:T(8,128)S(1)} %compare_select_fusion.16), kind=kOutput, calls=%fused_computation.66.clone.1 | convolution fusion | flops 163971072 | bytes 5566752 | tf_op jit(solution)/shard_map/while/body/eval_jaxpr/vmap(vmap())/dot_general | solution.py:82
  301.6 4.4 %multiply_reduce_fusion.6 = f32[8,9,128,128]{3,2,1,0:T(8,128)S(1)} fusion(f32[8,9,3]{2,1,0:T(8,128)S(1)} %copy.173, f32[8,9,3,128]{3,2,1,0:T(4,128)S(1)} %get-tuple-element.500, f32[8,3,128]{2,1,0:T(4,128)S(1)} %get-tuple-element.510), kind=kLoop, calls=%fused_computation.62.clone.1 | loop fusion | flops 12976128 | bytes 4842336 | tf_op jit(solution)/shard_map/while/body/eval_jaxpr/vmap(vmap())/reduce_sum | solution.py:35
  306.0 8.6 %fusion.96 = f32[8,9,11,128]{3,2,1,0:T(8,128)S(1)} fusion(f32[8,9,11,128]{3,2,1,0:T(8,128)S(1)} %concatenate.89, f32[8,9,128,128]{3,2,1,0:T(8,128)S(1)} %multiply_reduce_fusion.6, f32[8,9,128]{2,1,0:T(8,128)S(1)} %get-tuple-element.511, f32[8,9]{1,0:T(8,128)S(1)} %compare_select_fusion.16), kind=kOutput, calls=%fused_computation.66.clone.1 | convolution fusion | flops 163971072 | bytes 5566752 | tf_op jit(solution)/shard_map/while/body/eval_jaxpr/vmap(vmap())/dot_general | solution.py:82
  318.9 4.4 %multiply_reduce_fusion.6 = f32[8,9,128,128]{3,2,1,0:T(8,128)S(1)} fusion(f32[8,9,3]{2,1,0:T(8,128)S(1)} %copy.173, f32[8,9,3,128]{3,2,1,0:T(4,128)S(1)} %get-tuple-element.500, f32[8,3,128]{2,1,0:T(4,128)S(1)} %get-tuple-element.510), kind=kLoop, calls=%fused_computation.62.clone.1 | loop fusion | flops 12976128 | bytes 4842336 | tf_op jit(solution)/shard_map/while/body/eval_jaxpr/vmap(vmap())/reduce_sum | solution.py:35
  323.3 8.6 %fusion.96 = f32[8,9,11,128]{3,2,1,0:T(8,128)S(1)} fusion(f32[8,9,11,128]{3,2,1,0:T(8,128)S(1)} %concatenate.89, f32[8,9,128,128]{3,2,1,0:T(8,128)S(1)} %multiply_reduce_fusion.6, f32[8,9,128]{2,1,0:T(8,128)S(1)} %get-tuple-element.511, f32[8,9]{1,0:T(8,128)S(1)} %compare_select_fusion.16), kind=kOutput, calls=%fused_computation.66.clone.1 | convolution fusion | flops 163971072 | bytes 5566752 | tf_op jit(solution)/shard_map/while/body/eval_jaxpr/vmap(vmap())/dot_general | solution.py:82
  336.2 4.4 %multiply_reduce_fusion.6 = f32[8,9,128,128]{3,2,1,0:T(8,128)S(1)} fusion(f32[8,9,3]{2,1,0:T(8,128)S(1)} %copy.173, f32[8,9,3,128]{3,2,1,0:T(4,128)S(1)} %get-tuple-element.500, f32[8,3,128]{2,1,0:T(4,128)S(1)} %get-tuple-element.510), kind=kLoop, calls=%fused_computation.62.clone.1 | loop fusion | flops 12976128 | bytes 4842336 | tf_op jit(solution)/shard_map/while/body/eval_jaxpr/vmap(vmap())/reduce_sum | solution.py:35
  340.6 8.6 %fusion.96 = f32[8,9,11,128]{3,2,1,0:T(8,128)S(1)} fusion(f32[8,9,11,128]{3,2,1,0:T(8,128)S(1)} %concatenate.89, f32[8,9,128,128]{3,2,1,0:T(8,128)S(1)} %multiply_reduce_fusion.6, f32[8,9,128]{2,1,0:T(8,128)S(1)} %get-tuple-element.511, f32[8,9]{1,0:T(8,128)S(1)} %compare_select_fusion.16), kind=kOutput, calls=%fused_computation.66.clone.1 | convolution fusion | flops 163971072 | bytes 5566752 | tf_op jit(solution)/shard_map/while/body/eval_jaxpr/vmap(vmap())/dot_general | solution.py:82
  353.5 4.4 %multiply_reduce_fusion.6 = f32[8,9,128,128]{3,2,1,0:T(8,128)S(1)} fusion(f32[8,9,3]{2,1,0:T(8,128)S(1)} %copy.173, f32[8,9,3,128]{3,2,1,0:T(4,128)S(1)} %get-tuple-element.500, f32[8,3,128]{2,1,0:T(4,128)S(1)} %get-tuple-element.510), kind=kLoop, calls=%fused_computation.62.clone.1 | loop fusion | flops 12976128 | bytes 4842336 | tf_op jit(solution)/shard_map/while/body/eval_jaxpr/vmap(vmap())/reduce_sum | solution.py:35
  357.9 8.6 %fusion.96 = f32[8,9,11,128]{3,2,1,0:T(8,128)S(1)} fusion(f32[8,9,11,128]{3,2,1,0:T(8,128)S(1)} %concatenate.89, f32[8,9,128,128]{3,2,1,0:T(8,128)S(1)} %multiply_reduce_fusion.6, f32[8,9,128]{2,1,0:T(8,128)S(1)} %get-tuple-element.511, f32[8,9]{1,0:T(8,128)S(1)} %compare_select_fusion.16), kind=kOutput, calls=%fused_computation.66.clone.1 | convolution fusion | flops 163971072 | bytes 5566752 | tf_op jit(solution)/shard_map/while/body/eval_jaxpr/vmap(vmap())/dot_general | solution.py:82
  (516 shorter events, 57.3 us)
Async XLA Ops:
  4.1 22.0 %collective-permute-start.1 = (f32[9,1,2,128]{3,0,2,1:T(8,128)S(1)}, f32[9,1,2,128]{3,0,2,1:T(8,128)S(1)}, u32[]{:S(2)}, u32[]{:S(2)}) collective-permute-start(f32[9,1,2,128]{3,0,2,1:T(8,128)S(1)} %get-tuple-element.358), channel_id=1, source_target_pairs={{8,0},{16,8},{24,16},{32,24},{40,32},{48,40},{56,48},{64,56},{72,6... | collective-permute-start | bytes 27656 | tf_op jit(solution)/shard_map/ppermute | solution.py:26
  22.0 12.7 %collective-permute-start = (f32[9,1,2,128]{3,0,2,1:T(8,128)S(1)}, f32[9,1,2,128]{3,0,2,1:T(8,128)S(1)}, u32[]{:S(2)}, u32[]{:S(2)}) collective-permute-start(f32[9,1,2,128]{3,0,2,1:T(8,128)S(1)} %get-tuple-element.357), channel_id=1, source_target_pairs={{0,8},{8,16},{16,24},{24,32},{32,40},{40,48},{48,56},{56,64},{64,7... | collective-permute-start | bytes 27656 | tf_op jit(solution)/shard_map/ppermute | solution.py:24
  36.0 9.2 %collective-permute-start.3 = (f32[9,1,68,128]{3,1,2,0:T(1,128)S(1)}, f32[9,1,68,128]{3,1,2,0:T(1,128)S(1)}, u32[]{:S(2)}, u32[]{:S(2)}) collective-permute-start(f32[9,1,68,128]{3,1,2,0:T(1,128)S(1)} %copy.124), channel_id=1, source_target_pairs={{1,0},{2,1},{3,2},{4,3},{5,4},{6,5},{7,6},{0,7},{9,8},{10,9},{11,1... | collective-permute-start | bytes 940040 | tf_op jit(solution)/shard_map/ppermute | solution.py:26
  39.9 7.4 %collective-permute-start.2 = (f32[9,1,68,128]{3,1,2,0:T(1,128)S(1)}, f32[9,1,68,128]{3,1,2,0:T(1,128)S(1)}, u32[]{:S(2)}, u32[]{:S(2)}) collective-permute-start(f32[9,1,68,128]{3,1,2,0:T(1,128)S(1)} %copy.124), channel_id=1, source_target_pairs={{0,1},{1,2},{2,3},{3,4},{4,5},{5,6},{6,7},{7,0},{8,9},{9,10},{10,1... | collective-permute-start | bytes 940040 | tf_op jit(solution)/shard_map/ppermute | solution.py:24
  48.4 153.3 %copy-start = (f32[4,1,64,128]{3,2,1,0:T(8,128)S(1)}, f32[4,1,64,128]{3,2,1,0:T(8,128)}, u32[]{:S(2)}) copy-start(f32[4,1,64,128]{3,2,1,0:T(8,128)} %param.16) | copy-start | bytes 393220
  48.4 153.6 %copy-start.1 = (f32[1,64,128]{2,1,0:T(8,128)S(1)}, f32[1,64,128]{2,1,0:T(8,128)}, u32[]{:S(2)}) copy-start(f32[1,64,128]{2,1,0:T(8,128)} %param.19) | copy-start | bytes 98308
  48.4 153.6 %copy-start.2 = (f32[3]{0:T(128)S(1)}, f32[3]{0:T(128)}, u32[]{:S(2)}) copy-start(f32[3]{0:T(128)} %constant.339.clone) | copy-start | bytes 40
  203.1 9.4 %collective-permute-start.5 = (f32[4,1,2,128]{3,0,2,1:T(4,128)S(1)}, f32[4,1,2,128]{3,0,2,1:T(4,128)S(1)}, u32[]{:S(2)}, u32[]{:S(2)}) collective-permute-start(f32[4,1,2,128]{3,0,2,1:T(4,128)S(1)} %get-tuple-element.360), channel_id=1, source_target_pairs={{8,0},{16,8},{24,16},{32,24},{40,32},{48,40},{56,48},{64,56},{72,6... | collective-permute-start | bytes 12296 | tf_op jit(solution)/shard_map/ppermute | solution.py:26
  205.9 12.5 %collective-permute-start.4 = (f32[4,1,2,128]{3,0,2,1:T(4,128)S(1)}, f32[4,1,2,128]{3,0,2,1:T(4,128)S(1)}, u32[]{:S(2)}, u32[]{:S(2)}) collective-permute-start(f32[4,1,2,128]{3,0,2,1:T(4,128)S(1)} %get-tuple-element.359), channel_id=1, source_target_pairs={{0,8},{8,16},{16,24},{24,32},{32,40},{40,48},{48,56},{56,64},{64,7... | collective-permute-start | bytes 12296 | tf_op jit(solution)/shard_map/ppermute | solution.py:24
  218.5 8.7 %collective-permute-start.7 = (f32[4,1,68,128]{3,0,2,1:T(4,128)S(1)}, f32[4,1,68,128]{3,0,2,1:T(4,128)S(1)}, u32[]{:S(2)}, u32[]{:S(2)}) collective-permute-start(f32[4,1,68,128]{3,0,2,1:T(4,128)S(1)} %pad_maximum_fusion.2), channel_id=1, source_target_pairs={{1,0},{2,1},{3,2},{4,3},{5,4},{6,5},{7,6},{0,7},{9,8},{10,9},{11,1... | collective-permute-start | bytes 417800 | tf_op jit(solution)/shard_map/ppermute | solution.py:26
  224.5 3.9 %collective-permute-start.6 = (f32[4,1,68,128]{3,0,2,1:T(4,128)S(1)}, f32[4,1,68,128]{3,0,2,1:T(4,128)S(1)}, u32[]{:S(2)}, u32[]{:S(2)}) collective-permute-start(f32[4,1,68,128]{3,0,2,1:T(4,128)S(1)} %pad_maximum_fusion.2), channel_id=1, source_target_pairs={{0,1},{1,2},{2,3},{3,4},{4,5},{5,6},{6,7},{7,0},{8,9},{9,10},{10,1... | collective-permute-start | bytes 417800 | tf_op jit(solution)/shard_map/ppermute | solution.py:24
where the time goes:
time: 369 us; the launch traced here: 368 us
  matrix products  138 us (37%)
  other arithmetic  90.9 us (25%)
  local copies, waits for them, and re-layouts  60.7 us (16%)
  starting transfers between devices  43.6 us (12%)
  waiting for transfers between devices  20.6 us (6%)
  loops' own time  12.7 us (3%)
    reduce_sum x16, other arithmetic, kernel_matrix(): radius = jnp.sqrt(jnp.sum(delta * delta, axis=0))  70.5 us
    dot_general x8, matrix products, flux_pair(): jnp.dot(rows, link.T, precision=highest, preferred_element_type=jnp.float32)  69.2 us
    dot_general x8, matrix products, force_pair(): jnp.dot(rows, link.T, precision=highest, preferred_element_type=jnp.float32)  69.2 us
    ppermute x4, starting transfers between devices, padded(): lax.ppermute(head, axis, [((i + 1) % count, i) for i in range(count)])  30.7 us
    ppermute x4, waiting for transfers between devices, padded(): lax.ppermute(tail, axis, [(i, (i + 1) % count) for i in range(count)])  18 us
    concatenate x8, local copies, waits for them, and re-layouts, flux_pair(): jnp.concatenate([ones[None], conc_near, phi_near[None], conc_near * phi_n...  16 us
    ppermute x4, starting transfers between devices, padded(): lax.ppermute(tail, axis, [(i, (i + 1) % count) for i in range(count)])  12.9 us
    another operation x2, loops' own time, owner_sums(): lax.map(one_group, jnp.arange(count // step_tiles, dtype=jnp.int32))  12.7 us
  transfers between devices with their start and end apart: 8, of which 5 were waited for; matrix products, arithmetic and copies ran while one was open for 1% of the time, Pallas kernels for 0%

commit v1 on v0

v1 whole, which is shorter than its diff:
```python
from functools import partial

import jax
import jax.numpy as jnp
from jax import lax
from jax.experimental import pallas as pl
from jax.experimental.pallas import tpu as pltpu
from jax.sharding import PartitionSpec as P

support = 2.5
pair_scale = 1.0 / (support * support * support * 128.0)
time_step = 0.1
viscosity = 0.5
tiny = 1e-30
lanes = 128
halo = 4
rim = 2
slots = 9
inner = 3
near_rows = 24
flux_rows = 40
force_rows = 32
own_rows = 32
bf16 = jnp.bfloat16
f32 = jnp.float32
vmem_bytes = 24 * 1024 * 1024


def split(x):
    high = x.astype(bf16).astype(f32)
    return high, x - high


def split3(x):
    high, rest = split(x)
    mid, low = split(rest)
    return high, mid, low


def put(ref, tile, rows, row, value):
    ref[pl.ds(tile * rows + row, 8, stride=rows), :] = value


def get(ref, tile, rows, row):
    return ref[pl.ds(tile * rows + row, 8, stride=rows), :]


def shift_of(code):
    return (code // 3 - 2).astype(f32), (code % 3 - 1).astype(f32)


def fill_tables(add_ref, mul_ref):
    row = lax.broadcasted_iota(jnp.int32, (8, lanes), 0)
    for code in range(15):
        ox, oy = float(code // 3 - 2), float(code % 3 - 1)
        add = jnp.where(row < 4, jnp.where(row % 2 == 0, -2.0 * ox, -2.0 * oy), 1.0)
        add = jnp.where(row == 7, ox * ox + oy * oy, add)
        add_ref[code * 8 : code * 8 + 8, :] = add.astype(f32)
        mul_ref[code * 8 : code * 8 + 8, :] = jnp.where(
            row < 2, 2.0 * ox, jnp.where(row < 4, 2.0 * oy, 0.0)
        ).astype(f32)


def tile_index(step, count):
    return jnp.where(step < count + rim, step, step + 2 * (halo - rim))


def near_index(tile, code, count):
    span = count + 2 * halo
    signed = jnp.where(tile < count + halo, tile, tile - span)
    near = signed + code // 3 - 2
    near = jnp.where(near < 0, near + span, near)
    return code % 3 * span + near


def flux_kernel(
    count,
    codes_ref,
    wall_ref,
    param_ref,
    ext_ref,
    up_ref,
    down_ref,
    link_a,
    link_b,
    conc_ref,
    second_ref,
    near_ref,
    rows_ref,
    own_ref,
    sums_ref,
    add_ref,
    mul_ref,
    turn_ref,
    square_a,
    square_b,
):
    span = count + 2 * halo
    fill_tables(add_ref, mul_ref)
    row = lax.broadcasted_iota(jnp.int32, (8, lanes), 0)
    for code in range(15):
        ox, oy = float(code // 3 - 2), float(code % 3 - 1)
        turn_ref[code * 8 : code * 8 + 8, :] = jnp.where(row % 4 < 2, ox, oy).astype(f32)
    zero = jnp.zeros((8, lanes), f32)
    one = jnp.ones((8, lanes), f32)

    def prepare(strip, ref, is_own, chunk, carry):
        at = pl.multiple_of(chunk * 8, 8)
        load = lambda k: ref[k, pl.ds(at, 8), :]
        spot = [load(k) - 0.5 for k in range(3)]
        vol = load(3)
        conc = [load(4 + k) for k in range(4)]
        phi = load(8)
        parts = [split(s) for s in spot]
        high = [p[0] for p in parts]
        low = [p[1].astype(bf16).astype(f32) for p in parts]
        whole = [h + l for h, l in zip(high, low)]
        square = split3(whole[0] * whole[0] + whole[1] * whole[1] + whole[2] * whole[2])
        tile = strip * span + at
        near = [-2.0 * h for h in high] + [-2.0 * l for l in low]
        near = near + near + list(square) + [zero]
        near += [high[0], low[0], high[1], low[1], zero, zero, zero, zero]
        for k, value in enumerate(near):
            put(near_ref, tile, near_rows, k, value)
        vphi = vol * phi
        values = [vol] + [vol * c for c in conc] + [vphi] + [vphi * c for c in conc]
        values += [vol * w for w in whole] + [vphi * w for w in whole]
        pairs = [split(v) for v in values]
        flat = [p[0] for p in pairs] + [p[1] for p in pairs]
        for side in (0, 1):
            flat += [pairs[0][side], pairs[5][side]] * 2
        for k, value in enumerate(flat):
            put(rows_ref, tile, flux_rows, k, value)
        if is_own:
            mine = high + high + low + low + [one, one, one, zero]
            mine += [high[0], high[1], low[0], low[1]] + list(square) + [one]
            mine += [one, one, one, one, zero, zero, zero, zero]
            for k, value in enumerate(mine):
                put(own_ref, at, own_rows, k, value)
        return carry

    for strip, ref in ((0, up_ref), (1, ext_ref), (2, down_ref)):
        lax.fori_loop(0, span // 8, partial(prepare, strip, ref, strip == 1), 0)

    def squares(tile, firsts, square_ref, place):
        own = own_ref[pl.ds(pl.multiple_of(tile * own_rows, 8), own_rows), :].T.astype(bf16)
        for part, first in enumerate(firsts):
            near_all = []
            for k in range(inner):
                code = codes_ref[first + k]
                at = pl.multiple_of(near_index(tile, code, count) * near_rows, 8)
                table = pl.ds(pl.multiple_of(code * 8, 8), 8)
                near_all.append(
                    jnp.concatenate(
                        [
                            near_ref[pl.ds(at, 16), :],
                            add_ref[table, :],
                            near_ref[pl.ds(at + 16, 8), :] * mul_ref[table, :],
                        ],
                        axis=0,
                    ).astype(bf16)
                )
            square_ref[place + part] = jnp.dot(
                own, jnp.concatenate(near_all, axis=1), preferred_element_type=f32
            )

    def weigh(square_ref, link_ref, base, parts):
        for part in range(parts):
            square = jnp.maximum(square_ref[part], tiny)
            near = jnp.maximum(support - square * lax.rsqrt(square), 0.0)
            link_ref[base + part] = (near * near * near).astype(bf16)

    def moments(tile, firsts, link_ref, base):
        total = None
        for part, first in enumerate(firsts):
            rows_all = []
            for k in range(inner):
                code = codes_ref[first + k]
                at = pl.multiple_of(near_index(tile, code, count) * flux_rows, 8)
                turn = turn_ref[pl.ds(pl.multiple_of(code * 8, 8), 8), :]
                rows_all.append(
                    jnp.concatenate(
                        [rows_ref[pl.ds(at, 32), :], rows_ref[pl.ds(at + 32, 8), :] * turn, zero],
                        axis=0,
                    ).astype(bf16)
                )
            sums = lax.dot_general(
                jnp.concatenate(rows_all, axis=1),
                link_ref[base + part],
                (((1,), (1,)), ((), ())),
                preferred_element_type=f32,
            )
            total = sums if total is None else total + sums
        sums_ref[pl.ds(pl.multiple_of(tile * flux_rows, 8), flux_rows), :] = total[0:flux_rows]

    def pipeline(units, tiles_each, parts_each):
        last = units - 1

        def tiles(unit):
            for k in range(tiles_each):
                tile = tile_index(unit * tiles_each + k, count)
                yield k, tile, [tile * slots + part * inner for part in range(parts_each)]

        def stage_one(unit, square_ref):
            for k, tile, firsts in tiles(jnp.minimum(unit, last)):
                squares(tile, firsts, square_ref, k * parts_each)

        def stage_two(unit, square_ref, link_ref):
            weigh(square_ref, link_ref, unit // 2 * inner, tiles_each * parts_each)

        def stage_three(unit, link_ref):
            unit = jnp.maximum(unit, 0)
            for k, tile, firsts in tiles(unit):
                moments(tile, firsts, link_ref, unit // 2 * inner + k * parts_each)

        stage_one(0, square_a)

        def body(step, carry):
            unit = step * 2
            stage_one(unit + 1, square_b)
            stage_two(unit, square_a, link_a)
            stage_three(unit - 1, link_b)
            stage_one(unit + 2, square_a)
            stage_two(unit + 1, square_b, link_b)
            stage_three(unit, link_a)
            return carry

        lax.fori_loop(0, units // 2, body, 0)
        stage_three(last, link_b)

    @pl.when(wall_ref[0] == 1)
    def _():
        pipeline(count + 2 * rim, 1, slots // inner)

    @pl.when(wall_ref[0] == 0)
    def _():
        pipeline((count + 2 * rim) // 2, 2, 1)

    def finish(chunk, carry):
        at = pl.multiple_of(chunk * 8, 8)
        load = lambda k: ext_ref[k, pl.ds(at, 8), :]
        spot = [load(k) - 0.5 for k in range(3)]
        conc = [load(4 + k) for k in range(4)]
        phi = load(8)
        density = load(12)
        raw = [get(sums_ref, at, flux_rows, k) for k in range(flux_rows)]
        sums = [(raw[k] + raw[16 + k]) * pair_scale for k in range(16)]
        moved = [(raw[32 + k] + raw[36 + k]) * pair_scale for k in range(4)]
        total, link_phi = sums[0], sums[5]
        spread = link_phi - phi * total
        charge = zero
        press = zero
        for s in range(4):
            z = param_ref[4 + s]
            flux = 2.0 * (sums[1 + s] - conc[s] * total) + z * (
                conc[s] * spread + sums[6 + s] - phi * sums[1 + s]
            )
            fresh = conc[s] + time_step * param_ref[s] * flux
            conc_ref[s, pl.ds(at, 8), :] = fresh
            charge = charge + z * fresh
            press = press + fresh
        second_ref[0, pl.ds(at, 8), :] = press
        link_spot = [sums[10] + moved[0], sums[11] + moved[2], sums[12]]
        link_pspot = [sums[13] + moved[1], sums[14] + moved[3], sums[15]]
        push = time_step * charge / density
        for k in range(3):
            field = spot[k] * spread - (link_pspot[k] - phi * link_spot[k])
            if k == 0:
                field = field + 1.0
            second_ref[1 + k, pl.ds(at, 8), :] = load(9 + k) + push * field
        return carry

    lax.fori_loop(0, span // 8, finish, 0)


def force_kernel(
    count,
    codes_ref,
    wall_ref,
    ext_ref,
    up_ref,
    down_ref,
    second_ref,
    second_up_ref,
    second_down_ref,
    link_a,
    link_b,
    out_ref,
    rows_ref,
    sums_ref,
    turn_ref,
):
    span = count + 2 * halo
    row = lax.broadcasted_iota(jnp.int32, (16, lanes), 0)
    for code in range(15):
        ox, oy = float(code // 3 - 2), float(code % 3 - 1)
        turn_ref[code * 16 : code * 16 + 16, :] = jnp.where(
            row < 11, 1.0, jnp.where(row < 13, ox, jnp.where(row < 15, oy, 0.0))
        ).astype(f32)
    zero = jnp.zeros((8, lanes), f32)

    def prepare(strip, ref, ref_two, chunk, carry):
        at = pl.multiple_of(chunk * 8, 8)
        spot = [ref[k, pl.ds(at, 8), :] - 0.5 for k in range(3)]
        vol = ref[3, pl.ds(at, 8), :]
        press = ref_two[0, pl.ds(at, 8), :]
        speed = [ref_two[1 + k, pl.ds(at, 8), :] for k in range(3)]
        vpress = vol * press
        values = [vol] + [vol * w for w in spot] + [vpress] + [vpress * w for w in spot]
        values += [vol * w for w in speed]
        pairs = [split(v) for v in values]
        flat = []
        for side in (0, 1):
            flat += [p[side] for p in pairs] + [pairs[0][side], pairs[4][side]] * 2 + [zero]
        tile = strip * span + at
        for k, value in enumerate(flat):
            put(rows_ref, tile, force_rows, k, value)
        return carry

    for strip, ref, ref_two in (
        (0, up_ref, second_up_ref),
        (1, ext_ref, second_ref),
        (2, down_ref, second_down_ref),
    ):
        lax.fori_loop(0, span // 8, partial(prepare, strip, ref, ref_two), 0)

    def moments(tile, firsts, link_ref, base):
        total = None
        for part, first in enumerate(firsts):
            rows_all = []
            for k in range(inner):
                code = codes_ref[first + k]
                at = pl.multiple_of(near_index(tile, code, count) * force_rows, 8)
                turn = turn_ref[pl.ds(pl.multiple_of(code * 16, 8), 16), :]
                rows_all.append(
                    jnp.concatenate(
                        [rows_ref[pl.ds(at, 16), :] * turn, rows_ref[pl.ds(at + 16, 16), :] * turn],
                        axis=0,
                    ).astype(bf16)
                )
            sums = lax.dot_general(
                jnp.concatenate(rows_all, axis=1),
                link_ref[base + part],
                (((1,), (1,)), ((), ())),
                preferred_element_type=f32,
            )
            total = sums if total is None else total + sums
        sums_ref[pl.ds(pl.multiple_of(tile * 16, 8), 16), :] = total[0:16] + total[16:32]

    def sweep(steps, tiles_each, parts_each):
        def body(step, carry):
            for side, link_ref in enumerate((link_a, link_b)):
                for k in range(tiles_each):
                    tile = (step * 2 + side) * tiles_each + k
                    firsts = [tile * slots + part * inner for part in range(parts_each)]
                    moments(tile, firsts, link_ref, step * inner + k * parts_each)
            return carry

        lax.fori_loop(0, steps, body, 0)

    @pl.when(wall_ref[0] == 1)
    def _():
        sweep(count // 2, 1, slots // inner)

    @pl.when(wall_ref[0] == 0)
    def _():
        sweep(count // 4, 2, 1)

    def finish(chunk, carry):
        at = pl.multiple_of(chunk * 8, 8)
        spot = [ext_ref[k, pl.ds(at, 8), :] - 0.5 for k in range(3)]
        density = ext_ref[12, pl.ds(at, 8), :]
        press = second_ref[0, pl.ds(at, 8), :]
        sums = [get(sums_ref, at, 16, k) * pair_scale for k in range(15)]
        total = sums[0]
        link_spot = [sums[1] + sums[11], sums[2] + sums[13], sums[3]]
        link_pspot = [sums[5] + sums[12], sums[6] + sums[14], sums[7]]
        for k in range(3):
            speed = second_ref[1 + k, pl.ds(at, 8), :]
            push = press * (total * spot[k] - link_spot[k]) + spot[k] * sums[4] - link_pspot[k]
            drag = sums[8 + k] - speed * total
            accel = push / density + 2.0 * viscosity * drag
            out_ref[k, pl.ds(at, 8), :] = speed + time_step * accel
        return carry

    lax.fori_loop(0, count // 8, finish, 0)


def ring(axis, step, wrap):
    size = lax.axis_size(axis)
    pairs = [(i, i + step) for i in range(size)]
    if wrap:
        return [(i, j % size) for i, j in pairs]
    return [(i, j) for i, j in pairs if 0 <= j < size]


def per_device(offsets, velocity, conc, potential, mass, density, diffusivity, valence, pair_codes):
    count = offsets.shape[2]
    span = count + 2 * halo
    place = lax.axis_index("trans")
    wall = ((place == 0) | (place == lax.axis_size("trans") - 1)).astype(jnp.int32)[None]
    params = jnp.concatenate([diffusivity, valence.astype(f32)])
    codes = jnp.pad(pair_codes.astype(f32), ((0, 0), (0, 0), (0, lanes - slots)))
    own = jnp.concatenate(
        [offsets, (mass / density)[None], conc, potential[None], velocity, density[None], codes[None]],
        axis=0,
    )[:, 0]
    right = lax.ppermute(own[:, :halo], "stream", ring("stream", -1, True))
    left = lax.ppermute(own[:, count - halo :], "stream", ring("stream", 1, True))
    ext = jnp.concatenate([own, right, left], axis=1)
    mid = ext[0:9]
    up = lax.ppermute(mid, "trans", ring("trans", 1, False))
    down = lax.ppermute(mid, "trans", ring("trans", -1, False))
    listed = ext[13, :, :slots].astype(jnp.int32).reshape(-1)
    groups = (count + 2 * rim) // 2 * (slots // inner)
    smem = pl.BlockSpec(memory_space=pltpu.SMEM)
    vmem = pl.BlockSpec(memory_space=pltpu.VMEM)
    link_a, link_b, conc_ext, second = pl.pallas_call(
        partial(flux_kernel, count),
        out_shape=(
            pltpu.VMEM((groups, lanes, inner * lanes), bf16),
            pltpu.VMEM((groups, lanes, inner * lanes), bf16),
            jax.ShapeDtypeStruct((4, span, lanes), f32),
            jax.ShapeDtypeStruct((4, span, lanes), f32),
        ),
        in_specs=[smem, smem, smem, vmem, vmem, vmem],
        out_specs=(vmem,) * 4,
        scratch_shapes=[
            pltpu.VMEM((3 * span * near_rows, lanes), f32),
            pltpu.VMEM((3 * span * flux_rows, lanes), f32),
            pltpu.VMEM((span * own_rows, lanes), f32),
            pltpu.VMEM((span * flux_rows, lanes), f32),
            pltpu.VMEM((15 * 8, lanes), f32),
            pltpu.VMEM((15 * 8, lanes), f32),
            pltpu.VMEM((15 * 8, lanes), f32),
            pltpu.VMEM((inner, lanes, inner * lanes), f32),
            pltpu.VMEM((inner, lanes, inner * lanes), f32),
        ],
        compiler_params=pltpu.CompilerParams(vmem_limit_bytes=vmem_bytes),
    )(listed, wall, params, ext, up, down)
    second_up = lax.ppermute(second, "trans", ring("trans", 1, False))
    second_down = lax.ppermute(second, "trans", ring("trans", -1, False))
    velocity_new = pl.pallas_call(
        partial(force_kernel, count),
        out_shape=jax.ShapeDtypeStruct((3, count, lanes), f32),
        in_specs=[smem, smem] + [vmem] * 8,
        out_specs=vmem,
        scratch_shapes=[
            pltpu.VMEM((3 * span * force_rows, lanes), f32),
            pltpu.VMEM((count * 16, lanes), f32),
            pltpu.VMEM((15 * 16, lanes), f32),
        ],
        compiler_params=pltpu.CompilerParams(vmem_limit_bytes=vmem_bytes),
    )(
        listed,
        wall,
        ext,
        up,
        down,
        second,
        second_up,
        second_down,
        pltpu.with_memory_space_constraint(link_a, pltpu.VMEM),
        pltpu.with_memory_space_constraint(link_b, pltpu.VMEM),
    )
    return conc_ext[:, None, :count], velocity_new[:, None]


def solution(mesh):
    placed = (
        P(None, "trans", "stream", None),
        P(None, "trans", "stream", None),
        P(None, "trans", "stream", None),
        P("trans", "stream", None),
        P("trans", "stream", None),
        P("trans", "stream", None),
        P(),
        P(),
        P("trans", "stream", None),
    )
    return jax.shard_map(
        per_device,
        mesh=mesh,
        in_specs=placed,
        out_specs=(P(None, "trans", "stream", None), P(None, "trans", "stream", None)),
        check_vma=False,
    )
```

time: 369 us -> 92.8 us (0.25)
  the two profiles are of different devices: /device:TPU:1 before, /device:TPU:97 now
where the time goes in v1:
time: 92.8 us; the launch traced here: 92.2 us
  Pallas kernels  45.5 us (49%)
  starting transfers between devices  25.2 us (27%)
  waiting for transfers between devices  12.8 us (14%)
  local copies, waits for them, and re-layouts  5.86 us (6%)
  other arithmetic  2.23 us (2%)
    pallas_call x1, Pallas kernels, per_device(): pl.pallas_call(partial(flux_kernel, count), out_shape=(pltpu.VMEM((groups...  31.4 us
    ppermute x1, starting transfers between devices, per_device(): right = lax.ppermute(own[:, :halo], 'stream', ring('stream', -1, True))  14.4 us
    pallas_call x1, Pallas kernels, per_device(): pl.pallas_call(partial(force_kernel, count), out_shape=jax.ShapeDtypeStru...  14.1 us
    ppermute x1, waiting for transfers between devices, per_device(): lax.ppermute(own[:, count - halo:], 'stream', ring('stream', 1, True))  10.1 us
    unnamed x7, local copies, waits for them, and re-layouts  5.68 us
    ppermute x1, starting transfers between devices, per_device(): down = lax.ppermute(mid, 'trans', ring('trans', -1, False))  4.95 us
    ppermute x1, starting transfers between devices, per_device(): lax.ppermute(own[:, count - halo:], 'stream', ring('stream', 1, True))  1.92 us
  transfers between devices with their start and end apart: 6, of which 3 were waited for; matrix products, arithmetic and copies ran while one was open for 2% of the time, Pallas kernels for 0%

profile of v1, /device:TPU:97, one launch (start us, length us, event | category | flops | bytes accessed | tf_op | source)
XLA Modules:
  0.0 92.2 jit_solution(2230714896558642289)
XLA Ops:
  0.6 0.8 copy.17
  1.4 0.9 bitcast_dynamic-update-slice_fusion.2
  2.3 0.8 bitcast_dynamic-update-slice_fusion.6
  3.1 0.9 bitcast_dynamic-update-slice_fusion
  4.0 0.8 bitcast_dynamic-update-slice_fusion.5
  4.8 0.9 bitcast_dynamic-update-slice_fusion.1
  5.7 0.8 bitcast_dynamic-update-slice_fusion.4
  6.5 14.4 %collective-permute-start = (f32[14,4,128]{2,1,0:T(4,128)S(1)}, f32[14,4,128]{2,1,0:T(4,128)S(1)}, u32[]{:S(2)}, u32[]{:S(2)}) collective-permute-start(f32[14,4,128]{2,1,0:T(4,128)S(1)} %get-tuple-element.14), channel_id=1, source_target_pairs={{0,504},{8,0},{16,8},{24,16},{32,24},{40,32},{48,40},{56,48},{64,5... | collective-permute-start | bytes 86024 | tf_op jit(solution)/shard_map/ppermute | solution.py:408
  20.9 1.9 %collective-permute-start.1 = (f32[14,4,128]{2,1,0:T(4,128)S(1)}, f32[14,4,128]{2,1,0:T(4,128)S(1)}, u32[]{:S(2)}, u32[]{:S(2)}) collective-permute-start(f32[14,4,128]{2,1,0:T(4,128)S(1)} %get-tuple-element.15), channel_id=1, source_target_pairs={{0,8},{8,16},{16,24},{24,32},{32,40},{40,48},{48,56},{56,64},{64,7... | collective-permute-start | bytes 86024 | tf_op jit(solution)/shard_map/ppermute | solution.py:409
  22.8 0.7 convert_element_type.19
  23.5 0.0 collective-permute-done
  23.5 10.1 %collective-permute-done.1 = f32[14,4,128]{2,1,0:T(4,128)S(1)} collective-permute-done((f32[14,4,128]{2,1,0:T(4,128)S(1)}, f32[14,4,128]{2,1,0:T(4,128)S(1)}, u32[]{:S(2)}, u32[]{:S(2)}) %collective-permute-start.1) | collective-permute-done | bytes 28704 | tf_op jit(solution)/shard_map/ppermute | solution.py:409
  33.7 4.9 %collective-permute-start.3 = (f32[9,72,128]{2,1,0:T(8,128)S(1)}, f32[9,72,128]{2,1,0:T(8,128)S(1)}, u32[]{:S(2)}, u32[]{:S(2)}) collective-permute-start(f32[9,72,128]{2,1,0:T(8,128)S(1)} %slice.23), channel_id=1, source_target_pairs={{1,0},{2,1},{3,2},{4,3},{5,4},{6,5},{7,6},{9,8},{10,9},{11,10},{12... | collective-permute-start | bytes 995336 | tf_op jit(solution)/shard_map/ppermute | solution.py:413
  38.7 1.3 %collective-permute-start.2 = (f32[9,72,128]{2,1,0:T(8,128)S(1)}, f32[9,72,128]{2,1,0:T(8,128)S(1)}, u32[]{:S(2)}, u32[]{:S(2)}) collective-permute-start(f32[9,72,128]{2,1,0:T(8,128)S(1)} %slice.23), channel_id=1, source_target_pairs={{0,1},{1,2},{2,3},{3,4},{4,5},{5,6},{6,7},{8,9},{9,10},{10,11},{11... | collective-permute-start | bytes 995336 | tf_op jit(solution)/shard_map/ppermute | solution.py:412
  40.0 0.7 pad_maximum_fusion.1.param_ref
  40.7 0.1 convert_element_type.18.codes_ref
  40.8 0.0 collective-permute-done.3.down_ref
  40.9 1.3 %collective-permute-done.2.up_ref = f32[9,72,128]{2,1,0:T(8,128)S(1)} collective-permute-done((f32[9,72,128]{2,1,0:T(8,128)S(1)}, f32[9,72,128]{2,1,0:T(8,128)S(1)}, u32[]{:S(2)}, u32[]{:S(2)}) %collective-permute-start.2) | collective-permute-done | bytes 331808 | tf_op jit(solution)/shard_map/ppermute | solution.py:412
  42.2 31.4 %shard_map.104 = (bf16[102,128,384]{2,1,0:T(8,128)(2,1)S(1)}, bf16[102,128,384]{2,1,0:T(8,128)(2,1)S(1)}, f32[4,72,128]{2,1,0:T(8,128)S(1)}, f32[4,72,128]{2,1,0:T(8,128)S(1)}) custom-call(s32[648]{0:T(1024)S(1)} %convert_element_type.18.codes_ref, s32[1]{0:T(128)} %bitcast.8.wall_ref, f32[8]{0:T(128)S(1)} %pad_maximum_fusion.1.param_ref, ...), custom_call_target="tpu_custom_call" | custom-call | tf_op jit(solution)/shard_map/pallas_call | solution.py:418
  73.6 1.3 %collective-permute-start.5 = (f32[4,72,128]{2,1,0:T(8,128)S(1)}, f32[4,72,128]{2,1,0:T(8,128)S(1)}, u32[]{:S(2)}, u32[]{:S(2)}) collective-permute-start(f32[4,72,128]{2,1,0:T(8,128)S(1)} %get-tuple-element.7.second_ref), channel_id=1, source_target_pairs={{1,0},{2,1},{3,2},{4,3},{5,4},{6,5},{7,6},{9,8},{10,9},{11,10},{12... | collective-permute-start | bytes 442376 | tf_op jit(solution)/shard_map/ppermute | solution.py:442
  74.9 1.3 %collective-permute-start.4 = (f32[4,72,128]{2,1,0:T(8,128)S(1)}, f32[4,72,128]{2,1,0:T(8,128)S(1)}, u32[]{:S(2)}, u32[]{:S(2)}) collective-permute-start(f32[4,72,128]{2,1,0:T(8,128)S(1)} %get-tuple-element.7.second_ref), channel_id=1, source_target_pairs={{0,1},{1,2},{2,3},{3,4},{4,5},{5,6},{6,7},{8,9},{9,10},{10,11},{11... | collective-permute-start | bytes 442376 | tf_op jit(solution)/shard_map/ppermute | solution.py:441
  76.2 0.7 slice_bitcast_fusion
  76.8 0.0 collective-permute-done.5.second_down_ref
  76.8 1.3 %collective-permute-done.4.second_up_ref = f32[4,72,128]{2,1,0:T(8,128)S(1)} collective-permute-done((f32[4,72,128]{2,1,0:T(8,128)S(1)}, f32[4,72,128]{2,1,0:T(8,128)S(1)}, u32[]{:S(2)}, u32[]{:S(2)}) %collective-permute-start.4) | collective-permute-done | bytes 147488 | tf_op jit(solution)/shard_map/ppermute | solution.py:441
  78.1 14.1 %shard_map.105 = f32[3,64,128]{2,1,0:T(8,128)} custom-call(s32[648]{0:T(1024)S(1)} %convert_element_type.18.codes_ref, s32[1]{0:T(128)} %bitcast.8.wall_ref, f32[14,72,128]{2,1,0:T(8,128)S(1)} %pad_maximum_fusion.ext_ref, f32[9,72,128]{2,1,0:T(8,128)S(1)} %collective-permute-done.2.up_ref, f32[9,72,128]{2,1,0:T(8,128)S(1)} %collective-permute-done.3.down_ref, ...), custom_call_target="tpu_custom_call" | custom-call | tf_op jit(solution)/shard_map/pallas_call | solution.py:443
  (6 shorter events, 0.1 us)
Async XLA Ops:
  6.5 17.0 %collective-permute-start = (f32[14,4,128]{2,1,0:T(4,128)S(1)}, f32[14,4,128]{2,1,0:T(4,128)S(1)}, u32[]{:S(2)}, u32[]{:S(2)}) collective-permute-start(f32[14,4,128]{2,1,0:T(4,128)S(1)} %get-tuple-element.14), channel_id=1, source_target_pairs={{0,504},{8,0},{16,8},{24,16},{32,24},{40,32},{48,40},{56,48},{64,5... | collective-permute-start | bytes 86024 | tf_op jit(solution)/shard_map/ppermute | solution.py:408
  20.9 12.7 %collective-permute-start.1 = (f32[14,4,128]{2,1,0:T(4,128)S(1)}, f32[14,4,128]{2,1,0:T(4,128)S(1)}, u32[]{:S(2)}, u32[]{:S(2)}) collective-permute-start(f32[14,4,128]{2,1,0:T(4,128)S(1)} %get-tuple-element.15), channel_id=1, source_target_pairs={{0,8},{8,16},{16,24},{24,32},{32,40},{40,48},{48,56},{56,64},{64,7... | collective-permute-start | bytes 86024 | tf_op jit(solution)/shard_map/ppermute | solution.py:409
  33.7 7.1 %collective-permute-start.3 = (f32[9,72,128]{2,1,0:T(8,128)S(1)}, f32[9,72,128]{2,1,0:T(8,128)S(1)}, u32[]{:S(2)}, u32[]{:S(2)}) collective-permute-start(f32[9,72,128]{2,1,0:T(8,128)S(1)} %slice.23), channel_id=1, source_target_pairs={{1,0},{2,1},{3,2},{4,3},{5,4},{6,5},{7,6},{9,8},{10,9},{11,10},{12... | collective-permute-start | bytes 995336 | tf_op jit(solution)/shard_map/ppermute | solution.py:413
  38.7 3.5 %collective-permute-start.2 = (f32[9,72,128]{2,1,0:T(8,128)S(1)}, f32[9,72,128]{2,1,0:T(8,128)S(1)}, u32[]{:S(2)}, u32[]{:S(2)}) collective-permute-start(f32[9,72,128]{2,1,0:T(8,128)S(1)} %slice.23), channel_id=1, source_target_pairs={{0,1},{1,2},{2,3},{3,4},{4,5},{5,6},{6,7},{8,9},{9,10},{10,11},{11... | collective-permute-start | bytes 995336 | tf_op jit(solution)/shard_map/ppermute | solution.py:412
  73.6 3.3 %collective-permute-start.5 = (f32[4,72,128]{2,1,0:T(8,128)S(1)}, f32[4,72,128]{2,1,0:T(8,128)S(1)}, u32[]{:S(2)}, u32[]{:S(2)}) collective-permute-start(f32[4,72,128]{2,1,0:T(8,128)S(1)} %get-tuple-element.7.second_ref), channel_id=1, source_target_pairs={{1,0},{2,1},{3,2},{4,3},{5,4},{6,5},{7,6},{9,8},{10,9},{11,10},{12... | collective-permute-start | bytes 442376 | tf_op jit(solution)/shard_map/ppermute | solution.py:442
  74.9 3.3 %collective-permute-start.4 = (f32[4,72,128]{2,1,0:T(8,128)S(1)}, f32[4,72,128]{2,1,0:T(8,128)S(1)}, u32[]{:S(2)}, u32[]{:S(2)}) collective-permute-start(f32[4,72,128]{2,1,0:T(8,128)S(1)} %get-tuple-element.7.second_ref), channel_id=1, source_target_pairs={{0,1},{1,2},{2,3},{3,4},{4,5},{5,6},{6,7},{8,9},{9,10},{10,11},{11... | collective-permute-start | bytes 442376 | tf_op jit(solution)/shard_map/ppermute | solution.py:441

commit v2 on v1

--- a/solution.py
+++ b/solution.py
@@ -45,10 +45,6 @@
     return ref[pl.ds(tile * rows + row, 8, stride=rows), :]
 
 
-def shift_of(code):
-    return (code // 3 - 2).astype(f32), (code % 3 - 1).astype(f32)
-
-
 def fill_tables(add_ref, mul_ref):
     row = lax.broadcasted_iota(jnp.int32, (8, lanes), 0)
     for code in range(15):
@@ -65,12 +61,21 @@
     return jnp.where(step < count + rim, step, step + 2 * (halo - rim))
 
 
-def near_index(tile, code, count):
+def packed_list(codes, count):
     span = count + 2 * halo
-    signed = jnp.where(tile < count + halo, tile, tile - span)
-    near = signed + code // 3 - 2
+    tile = jnp.arange(span, dtype=jnp.int32)[:, None]
+    near = jnp.where(tile < count + halo, tile, tile - span) + codes // 3 - 2
     near = jnp.where(near < 0, near + span, near)
-    return code % 3 * span + near
+    return ((codes % 3 * span + near) * 16 + codes).reshape(-1)
+
+
+def unpack(value, rows, table_rows):
+    at = pl.multiple_of((value >> 4) * rows, 8)
+    return at, pl.ds(pl.multiple_of((value & 15) * table_rows, 8), table_rows)
+
+
+def used(wall_ref, strip):
+    return (wall_ref[0] == 0) | (wall_ref[1] == strip - 1)
 
 
 def flux_kernel(
@@ -139,17 +144,19 @@
                 put(own_ref, at, own_rows, k, value)
         return carry
 
-    for strip, ref in ((0, up_ref), (1, ext_ref), (2, down_ref)):
-        lax.fori_loop(0, span // 8, partial(prepare, strip, ref, strip == 1), 0)
+    lax.fori_loop(0, span // 8, partial(prepare, 1, ext_ref, True), 0)
+    for strip, ref in ((0, up_ref), (2, down_ref)):
+
+        @pl.when(used(wall_ref, strip))
+        def _():
+            lax.fori_loop(0, span // 8, partial(prepare, strip, ref, False), 0)
 
     def squares(tile, firsts, square_ref, place):
         own = own_ref[pl.ds(pl.multiple_of(tile * own_rows, 8), own_rows), :].T.astype(bf16)
         for part, first in enumerate(firsts):
             near_all = []
             for k in range(inner):
-                code = codes_ref[first + k]
-                at = pl.multiple_of(near_index(tile, code, count) * near_rows, 8)
-                table = pl.ds(pl.multiple_of(code * 8, 8), 8)
+                at, table = unpack(codes_ref[first + k], near_rows, 8)
                 near_all.append(
                     jnp.concatenate(
                         [
@@ -175,9 +182,8 @@
         for part, first in enumerate(firsts):
             rows_all = []
             for k in range(inner):
-                code = codes_ref[first + k]
-                at = pl.multiple_of(near_index(tile, code, count) * flux_rows, 8)
-                turn = turn_ref[pl.ds(pl.multiple_of(code * 8, 8), 8), :]
+                at, table = unpack(codes_ref[first + k], flux_rows, 8)
+                turn = turn_ref[table, :]
                 rows_all.append(
                     jnp.concatenate(
                         [rows_ref[pl.ds(at, 32), :], rows_ref[pl.ds(at + 32, 8), :] * turn, zero],
@@ -317,21 +323,20 @@
             put(rows_ref, tile, force_rows, k, value)
         return carry
 
-    for strip, ref, ref_two in (
-        (0, up_ref, second_up_ref),
-        (1, ext_ref, second_ref),
-        (2, down_ref, second_down_ref),
-    ):
-        lax.fori_loop(0, span // 8, partial(prepare, strip, ref, ref_two), 0)
+    lax.fori_loop(0, span // 8, partial(prepare, 1, ext_ref, second_ref), 0)
+    for strip, ref, ref_two in ((0, up_ref, second_up_ref), (2, down_ref, second_down_ref)):
+
+        @pl.when(used(wall_ref, strip))
+        def _():
+            lax.fori_loop(0, span // 8, partial(prepare, strip, ref, ref_two), 0)
 
     def moments(tile, firsts, link_ref, base):
         total = None
         for part, first in enumerate(firsts):
             rows_all = []
             for k in range(inner):
-                code = codes_ref[first + k]
-                at = pl.multiple_of(near_index(tile, code, count) * force_rows, 8)
-                turn = turn_ref[pl.ds(pl.multiple_of(code * 16, 8), 16), :]
+                at, table = unpack(codes_ref[first + k], force_rows, 16)
+                turn = turn_ref[table, :]
                 rows_all.append(
                     jnp.concatenate(
                         [rows_ref[pl.ds(at, 16), :] * turn, rows_ref[pl.ds(at + 16, 16), :] * turn],
@@ -386,35 +391,85 @@
     lax.fori_loop(0, count // 8, finish, 0)
 
 
-def ring(axis, step, wrap):
+def pack_kernel(
+    even_ref,
+    offsets_ref,
+    velocity_ref,
+    conc_ref,
+    phi_ref,
+    mass_ref,
+    density_ref,
+    codes_ref,
+    own_ref,
+    first_ref,
+    second_ref,
+):
+    count = offsets_ref.shape[1]
+    own_ref[0:3] = offsets_ref[...]
+    own_ref[3] = mass_ref[...] / density_ref[...]
+    own_ref[4:8] = conc_ref[...]
+    own_ref[8] = phi_ref[...]
+    own_ref[9:12] = velocity_ref[...]
+    own_ref[12] = density_ref[...]
+    codes = [codes_ref[k].astype(f32) for k in range(slots)]
+    own_ref[13] = jnp.concatenate(codes + [jnp.zeros((lanes - slots, count), f32)], axis=0).T
+    head = own_ref[:, 0:halo, :]
+    tail = own_ref[:, count - halo : count, :]
+    even = even_ref[0] == 1
+    first_ref[...] = jnp.where(even, tail, head)
+    second_ref[...] = jnp.where(even, head, tail)
+
+
+def swaps(axis, start):
     size = lax.axis_size(axis)
-    pairs = [(i, i + step) for i in range(size)]
-    if wrap:
-        return [(i, j % size) for i, j in pairs]
-    return [(i, j) for i, j in pairs if 0 <= j < size]
+    pairs = [(i, (i + 1) % size) for i in range(start, size, 2)]
+    return pairs + [(j, i) for i, j in pairs]
+
+
+def ring(axis, step):
+    size = lax.axis_size(axis)
+    return [(i, i + step) for i in range(size) if 0 <= i + step < size]
 
 
 def per_device(offsets, velocity, conc, potential, mass, density, diffusivity, valence, pair_codes):
     count = offsets.shape[2]
     span = count + 2 * halo
     place = lax.axis_index("trans")
-    wall = ((place == 0) | (place == lax.axis_size("trans") - 1)).astype(jnp.int32)[None]
+    last = lax.axis_size("trans") - 1
+    wall = jnp.stack([(place == 0) | (place == last), jnp.where(place == 0, 1, -1)]).astype(jnp.int32)
     params = jnp.concatenate([diffusivity, valence.astype(f32)])
-    codes = jnp.pad(pair_codes.astype(f32), ((0, 0), (0, 0), (0, lanes - slots)))
-    own = jnp.concatenate(
-        [offsets, (mass / density)[None], conc, potential[None], velocity, density[None], codes[None]],
-        axis=0,
-    )[:, 0]
-    right = lax.ppermute(own[:, :halo], "stream", ring("stream", -1, True))
-    left = lax.ppermute(own[:, count - halo :], "stream", ring("stream", 1, True))
+    smem = pl.BlockSpec(memory_space=pltpu.SMEM)
+    vmem = pl.BlockSpec(memory_space=pltpu.VMEM)
+    even = lax.axis_index("stream") % 2 == 0
+    own, first, other = pl.pallas_call(
+        pack_kernel,
+        out_shape=(
+            jax.ShapeDtypeStruct((14, count, lanes), f32),
+            jax.ShapeDtypeStruct((14, halo, lanes), f32),
+            jax.ShapeDtypeStruct((14, halo, lanes), f32),
+        ),
+        in_specs=[smem] + [vmem] * 7,
+        out_specs=(vmem,) * 3,
+    )(
+        even.astype(jnp.int32)[None],
+        offsets[:, 0],
+        velocity[:, 0],
+        conc[:, 0],
+        potential[0],
+        mass[0],
+        density[0],
+        pair_codes.transpose(2, 0, 1),
+    )
+    first = lax.ppermute(first, "stream", swaps("stream", 0))
+    other = lax.ppermute(other, "stream", swaps("stream", 1))
+    right = jnp.where(even, first, other)
+    left = jnp.where(even, other, first)
     ext = jnp.concatenate([own, right, left], axis=1)
     mid = ext[0:9]
-    up = lax.ppermute(mid, "trans", ring("trans", 1, False))
-    down = lax.ppermute(mid, "trans", ring("trans", -1, False))
-    listed = ext[13, :, :slots].astype(jnp.int32).reshape(-1)
+    up = lax.ppermute(mid, "trans", ring("trans", 1))
+    down = lax.ppermute(mid, "trans", ring("trans", -1))
+    listed = packed_list(ext[13, :, :slots].astype(jnp.int32), count)
     groups = (count + 2 * rim) // 2 * (slots // inner)
-    smem = pl.BlockSpec(memory_space=pltpu.SMEM)
-    vmem = pl.BlockSpec(memory_space=pltpu.VMEM)
     link_a, link_b, conc_ext, second = pl.pallas_call(
         partial(flux_kernel, count),
         out_shape=(
@@ -438,8 +493,8 @@
         ],
         compiler_params=pltpu.CompilerParams(vmem_limit_bytes=vmem_bytes),
     )(listed, wall, params, ext, up, down)
-    second_up = lax.ppermute(second, "trans", ring("trans", 1, False))
-    second_down = lax.ppermute(second, "trans", ring("trans", -1, False))
+    second_up = lax.ppermute(second, "trans", ring("trans", 1))
+    second_down = lax.ppermute(second, "trans", ring("trans", -1))
     velocity_new = pl.pallas_call(
         partial(force_kernel, count),
         out_shape=jax.ShapeDtypeStruct((3, count, lanes), f32),

time: 92.8 us -> 82.7 us (0.89)
  waiting for transfers between devices: 12.8 us -> 4.43 us
  local copies, waits for them, and re-layouts: 5.86 us -> 1.04 us
  starting transfers between devices: 25.2 us -> 27.4 us
    ppermute x6, waiting for transfers between devices: 12.8 us -> 4.43 us  [the longest x1 2.04 us: per_device(): up = lax.ppermute(mid, 'trans', ring('trans', 1))]
    unnamed x7 -> x1, local copies, waits for them, and re-layouts: 5.68 us -> 0.66 us
    ppermute x6, starting transfers between devices: 25.2 us -> 27.4 us  [the longest x1 10.8 us: per_device(): other = lax.ppermute(other, 'stream', swaps('stream', 1))]
    pallas_call x0 -> x1, Pallas kernels: none -> 1.91 us  [per_device(): pl.pallas_call(pack_kernel, out_shape=(jax.ShapeDtypeStruct((14, count, l...]
    concatenate x1, other arithmetic: 0.04 us -> 1.06 us  [per_device(): ext = jnp.concatenate([own, right, left], axis=1)]
  transfers between devices with their start and end apart: 6 -> 6, of which waited for: 3 -> 3; matrix products, arithmetic and copies ran while one was open for 2% -> 3% of each run, Pallas kernels for 0% -> 0%
where the time goes in v2:
time: 82.7 us; the launch traced here: 82.4 us
  Pallas kernels  46.2 us (56%)
  starting transfers between devices  27.4 us (33%)
  waiting for transfers between devices  4.43 us (5%)
  other arithmetic  2.56 us (3%)
  local copies, waits for them, and re-layouts  1.04 us (1%)
    pallas_call x1, Pallas kernels, per_device(): pl.pallas_call(partial(flux_kernel, count), out_shape=(pltpu.VMEM((groups...  30.9 us
    pallas_call x1, Pallas kernels, per_device(): pl.pallas_call(partial(force_kernel, count), out_shape=jax.ShapeDtypeStru...  13.4 us
    ppermute x1, starting transfers between devices, per_device(): other = lax.ppermute(other, 'stream', swaps('stream', 1))  10.8 us
    ppermute x1, starting transfers between devices, per_device(): first = lax.ppermute(first, 'stream', swaps('stream', 0))  8.81 us
    ppermute x1, starting transfers between devices, per_device(): down = lax.ppermute(mid, 'trans', ring('trans', -1))  3.94 us
    ppermute x1, waiting for transfers between devices, per_device(): up = lax.ppermute(mid, 'trans', ring('trans', 1))  2.04 us
    pallas_call x1, Pallas kernels, per_device(): pl.pallas_call(pack_kernel, out_shape=(jax.ShapeDtypeStruct((14, count, l...  1.91 us
  transfers between devices with their start and end apart: 6, of which 3 were waited for; matrix products, arithmetic and copies ran while one was open for 3% of the time, Pallas kernels for 0%

profile of v2, /device:TPU:97, one launch (start us, length us, event | category | flops | bytes accessed | tf_op | source)
XLA Modules:
  0.0 82.4 jit_solution(1292399890429627735)
XLA Ops:
  0.6 1.9 %shard_map.104 = (f32[14,64,128]{2,1,0:T(8,128)}, f32[14,4,128]{2,1,0:T(4,128)}, f32[14,4,128]{2,1,0:T(4,128)}) custom-call(s32[1]{0:T(128)} %bitcast.even_ref, f32[3,64,128]{2,1,0:T(8,128)} %bitcast.25, f32[3,64,128]{2,1,0:T(8,128)} %bitcast.26, f32[4,64,128]{2,1,0:T(8,128)} %bitcast.21, f32[64,128]{1,0:T(8,128)} %bitcast.27, f32[64,128]{1,0:T(8,128)} %bitcast.28, ...), custom_call_target="tpu_custom_call" | custom-call | tf_op jit(solution)/shard_map/pallas_call | solution.py:444
  2.6 8.8 %collective-permute-start = (f32[14,4,128]{2,1,0:T(4,128)}, f32[14,4,128]{2,1,0:T(4,128)S(1)}, u32[]{:S(2)}, u32[]{:S(2)}) collective-permute-start(f32[14,4,128]{2,1,0:T(4,128)} %get-tuple-element.10), channel_id=1, source_target_pairs={{0,8},{16,24},{32,40},{48,56},{64,72},{80,88},{96,104},{112,120},{... | collective-permute-start | bytes 86024 | tf_op jit(solution)/shard_map/ppermute | solution.py:463
  11.4 10.8 %collective-permute-start.1 = (f32[14,4,128]{2,1,0:T(4,128)}, f32[14,4,128]{2,1,0:T(4,128)S(1)}, u32[]{:S(2)}, u32[]{:S(2)}) collective-permute-start(f32[14,4,128]{2,1,0:T(4,128)} %get-tuple-element.11), channel_id=1, source_target_pairs={{8,16},{24,32},{40,48},{56,64},{72,80},{88,96},{104,112},{120,128}... | collective-permute-start | bytes 86024 | tf_op jit(solution)/shard_map/ppermute | solution.py:464
  22.2 0.7 convert_element_type.14
  22.8 0.1 pad_add_fusion.wall_ref
  22.9 0.7 pad_maximum_fusion.1.param_ref
  23.6 0.1 add.50
  23.7 0.1 add.51
  23.9 0.0 collective-permute-done
  23.9 1.1 %collective-permute-done.1 = f32[14,4,128]{2,1,0:T(4,128)S(1)} collective-permute-done((f32[14,4,128]{2,1,0:T(4,128)}, f32[14,4,128]{2,1,0:T(4,128)S(1)}, u32[]{:S(2)}, u32[]{:S(2)}) %collective-permute-start.1) | collective-permute-done | bytes 28704 | tf_op jit(solution)/shard_map/ppermute | solution.py:464
  25.0 1.1 %pad_maximum_fusion.ext_ref = f32[14,72,128]{2,1,0:T(8,128)S(1)} fusion(f32[14,4,128]{2,1,0:T(4,128)S(1)} %bitcast.23, f32[14,4,128]{2,1,0:T(4,128)S(1)} %bitcast.22, f32[14,64,128]{2,1,0:T(8,128)} %get-tuple-element.9), kind=kLoop, calls=%fused_computation | loop fusion | flops 258048 | bytes 1032192 | tf_op jit(solution)/shard_map/concatenate | solution.py:467
  26.1 3.9 %collective-permute-start.3 = (f32[9,72,128]{2,1,0:T(8,128)S(1)}, f32[9,72,128]{2,1,0:T(8,128)S(1)}, u32[]{:S(2)}, u32[]{:S(2)}) collective-permute-start(f32[9,72,128]{2,1,0:T(8,128)S(1)} %slice.13), channel_id=1, source_target_pairs={{1,0},{2,1},{3,2},{4,3},{5,4},{6,5},{7,6},{9,8},{10,9},{11,10},{12... | collective-permute-start | bytes 995336 | tf_op jit(solution)/shard_map/ppermute | solution.py:470
  30.0 1.3 %collective-permute-start.2 = (f32[9,72,128]{2,1,0:T(8,128)S(1)}, f32[9,72,128]{2,1,0:T(8,128)S(1)}, u32[]{:S(2)}, u32[]{:S(2)}) collective-permute-start(f32[9,72,128]{2,1,0:T(8,128)S(1)} %slice.13), channel_id=1, source_target_pairs={{0,1},{1,2},{2,3},{3,4},{4,5},{5,6},{6,7},{8,9},{9,10},{10,11},{11... | collective-permute-start | bytes 995336 | tf_op jit(solution)/shard_map/ppermute | solution.py:469
  31.3 0.1 convert_element_type.13
  31.5 0.0 collective-permute-done.3.down_ref
  31.5 2.0 %collective-permute-done.2.up_ref = f32[9,72,128]{2,1,0:T(8,128)S(1)} collective-permute-done((f32[9,72,128]{2,1,0:T(8,128)S(1)}, f32[9,72,128]{2,1,0:T(8,128)S(1)}, u32[]{:S(2)}, u32[]{:S(2)}) %collective-permute-start.2) | collective-permute-done | bytes 331808 | tf_op jit(solution)/shard_map/ppermute | solution.py:469
  33.5 30.9 %shard_map.105 = (bf16[102,128,384]{2,1,0:T(8,128)(2,1)S(1)}, bf16[102,128,384]{2,1,0:T(8,128)(2,1)S(1)}, f32[4,72,128]{2,1,0:T(8,128)S(1)}, f32[4,72,128]{2,1,0:T(8,128)S(1)}) custom-call(s32[648]{0:T(1024)S(1)} %fusion.3.codes_ref, s32[2]{0:T(128)S(1)} %pad_add_fusion.wall_ref, f32[8]{0:T(128)S(1)} %pad_maximum_fusion.1.param_ref, ...), custom_call_target="tpu_custom_call" | custom-call | tf_op jit(solution)/shard_map/pallas_call | solution.py:473
  64.4 1.3 %collective-permute-start.5 = (f32[4,72,128]{2,1,0:T(8,128)S(1)}, f32[4,72,128]{2,1,0:T(8,128)S(1)}, u32[]{:S(2)}, u32[]{:S(2)}) collective-permute-start(f32[4,72,128]{2,1,0:T(8,128)S(1)} %get-tuple-element.13.second_ref), channel_id=1, source_target_pairs={{1,0},{2,1},{3,2},{4,3},{5,4},{6,5},{7,6},{9,8},{10,9},{11,10},{12... | collective-permute-start | bytes 442376 | tf_op jit(solution)/shard_map/ppermute | solution.py:497
  65.7 1.3 %collective-permute-start.4 = (f32[4,72,128]{2,1,0:T(8,128)S(1)}, f32[4,72,128]{2,1,0:T(8,128)S(1)}, u32[]{:S(2)}, u32[]{:S(2)}) collective-permute-start(f32[4,72,128]{2,1,0:T(8,128)S(1)} %get-tuple-element.13.second_ref), channel_id=1, source_target_pairs={{0,1},{1,2},{2,3},{3,4},{4,5},{5,6},{6,7},{8,9},{9,10},{10,11},{11... | collective-permute-start | bytes 442376 | tf_op jit(solution)/shard_map/ppermute | solution.py:496
  67.0 0.7 slice_bitcast_fusion
  67.7 0.0 collective-permute-done.5.second_down_ref
  67.7 1.3 %collective-permute-done.4.second_up_ref = f32[4,72,128]{2,1,0:T(8,128)S(1)} collective-permute-done((f32[4,72,128]{2,1,0:T(8,128)S(1)}, f32[4,72,128]{2,1,0:T(8,128)S(1)}, u32[]{:S(2)}, u32[]{:S(2)}) %collective-permute-start.4) | collective-permute-done | bytes 147488 | tf_op jit(solution)/shard_map/ppermute | solution.py:496
  69.0 13.4 %shard_map.106 = f32[3,64,128]{2,1,0:T(8,128)} custom-call(s32[648]{0:T(1024)S(1)} %fusion.3.codes_ref, s32[2]{0:T(128)S(1)} %pad_add_fusion.wall_ref, f32[14,72,128]{2,1,0:T(8,128)S(1)} %pad_maximum_fusion.ext_ref, f32[9,72,128]{2,1,0:T(8,128)S(1)} %collective-permute-done.2.up_ref, f32[9,72,128]{2,1,0:T(8,128)S(1)} %collective-permute-done.3.down_ref, ...), custom_call_target="tpu_custom_call" | custom-call | tf_op jit(solution)/shard_map/pallas_call | solution.py:498
  (5 shorter events, 0.1 us)
Async XLA Ops:
  2.6 21.3 %collective-permute-start = (f32[14,4,128]{2,1,0:T(4,128)}, f32[14,4,128]{2,1,0:T(4,128)S(1)}, u32[]{:S(2)}, u32[]{:S(2)}) collective-permute-start(f32[14,4,128]{2,1,0:T(4,128)} %get-tuple-element.10), channel_id=1, source_target_pairs={{0,8},{16,24},{32,40},{48,56},{64,72},{80,88},{96,104},{112,120},{... | collective-permute-start | bytes 86024 | tf_op jit(solution)/shard_map/ppermute | solution.py:463
  11.4 13.6 %collective-permute-start.1 = (f32[14,4,128]{2,1,0:T(4,128)}, f32[14,4,128]{2,1,0:T(4,128)S(1)}, u32[]{:S(2)}, u32[]{:S(2)}) collective-permute-start(f32[14,4,128]{2,1,0:T(4,128)} %get-tuple-element.11), channel_id=1, source_target_pairs={{8,16},{24,32},{40,48},{56,64},{72,80},{88,96},{104,112},{120,128}... | collective-permute-start | bytes 86024 | tf_op jit(solution)/shard_map/ppermute | solution.py:464
  26.1 5.4 %collective-permute-start.3 = (f32[9,72,128]{2,1,0:T(8,128)S(1)}, f32[9,72,128]{2,1,0:T(8,128)S(1)}, u32[]{:S(2)}, u32[]{:S(2)}) collective-permute-start(f32[9,72,128]{2,1,0:T(8,128)S(1)} %slice.13), channel_id=1, source_target_pairs={{1,0},{2,1},{3,2},{4,3},{5,4},{6,5},{7,6},{9,8},{10,9},{11,10},{12... | collective-permute-start | bytes 995336 | tf_op jit(solution)/shard_map/ppermute | solution.py:470
  30.0 3.5 %collective-permute-start.2 = (f32[9,72,128]{2,1,0:T(8,128)S(1)}, f32[9,72,128]{2,1,0:T(8,128)S(1)}, u32[]{:S(2)}, u32[]{:S(2)}) collective-permute-start(f32[9,72,128]{2,1,0:T(8,128)S(1)} %slice.13), channel_id=1, source_target_pairs={{0,1},{1,2},{2,3},{3,4},{4,5},{5,6},{6,7},{8,9},{9,10},{10,11},{11... | collective-permute-start | bytes 995336 | tf_op jit(solution)/shard_map/ppermute | solution.py:469
  64.4 3.3 %collective-permute-start.5 = (f32[4,72,128]{2,1,0:T(8,128)S(1)}, f32[4,72,128]{2,1,0:T(8,128)S(1)}, u32[]{:S(2)}, u32[]{:S(2)}) collective-permute-start(f32[4,72,128]{2,1,0:T(8,128)S(1)} %get-tuple-element.13.second_ref), channel_id=1, source_target_pairs={{1,0},{2,1},{3,2},{4,3},{5,4},{6,5},{7,6},{9,8},{10,9},{11,10},{12... | collective-permute-start | bytes 442376 | tf_op jit(solution)/shard_map/ppermute | solution.py:497
  65.7 3.3 %collective-permute-start.4 = (f32[4,72,128]{2,1,0:T(8,128)S(1)}, f32[4,72,128]{2,1,0:T(8,128)S(1)}, u32[]{:S(2)}, u32[]{:S(2)}) collective-permute-start(f32[4,72,128]{2,1,0:T(8,128)S(1)} %get-tuple-element.13.second_ref), channel_id=1, source_target_pairs={{0,1},{1,2},{2,3},{3,4},{4,5},{5,6},{6,7},{8,9},{9,10},{10,11},{11... | collective-permute-start | bytes 442376 | tf_op jit(solution)/shard_map/ppermute | solution.py:496

commit v3 on v2

--- a/solution.py
+++ b/solution.py
@@ -16,7 +16,8 @@
 halo = 4
 rim = 2
 slots = 9
-inner = 3
+wall_parts = ((0, 2), (2, 2), (4, 2), (6, 2), (8, 1))
+inner_parts = ((0, 2), (2, 1))
 near_rows = 24
 flux_rows = 40
 force_rows = 32
@@ -72,6 +73,16 @@
 def unpack(value, rows, table_rows):
     at = pl.multiple_of((value >> 4) * rows, 8)
     return at, pl.ds(pl.multiple_of((value & 15) * table_rows, 8), table_rows)
+
+
+def blocks(first, many):
+    return slice(first * lanes, (first + many) * lanes)
+
+
+def in_turns(*stages):
+    stages = list(stages)
+    while stages:
+        stages = [stage for stage in stages if next(stage, stages) is None]
 
 
 def used(wall_ref, strip):
@@ -151,12 +162,12 @@
         def _():
             lax.fori_loop(0, span // 8, partial(prepare, strip, ref, False), 0)
 
-    def squares(tile, firsts, square_ref, place):
+    def squares(tile, square_ref, parts, lane):
         own = own_ref[pl.ds(pl.multiple_of(tile * own_rows, 8), own_rows), :].T.astype(bf16)
-        for part, first in enumerate(firsts):
+        for first, pairs in parts:
             near_all = []
-            for k in range(inner):
-                at, table = unpack(codes_ref[first + k], near_rows, 8)
+            for k in range(first, first + pairs):
+                at, table = unpack(codes_ref[tile * slots + k], near_rows, 8)
                 near_all.append(
                     jnp.concatenate(
                         [
@@ -167,80 +178,88 @@
                         axis=0,
                     ).astype(bf16)
                 )
-            square_ref[place + part] = jnp.dot(
+            square_ref[:, blocks(lane + first, pairs)] = jnp.dot(
                 own, jnp.concatenate(near_all, axis=1), preferred_element_type=f32
             )
-
-    def weigh(square_ref, link_ref, base, parts):
-        for part in range(parts):
-            square = jnp.maximum(square_ref[part], tiny)
-            near = jnp.maximum(support - square * lax.rsqrt(square), 0.0)
-            link_ref[base + part] = (near * near * near).astype(bf16)
-
-    def moments(tile, firsts, link_ref, base):
+            yield
+
+    def weigh(square_ref, link_ref, base, parts, lane):
+        for first, pairs in parts:
+            for k in range(lane + first, lane + first + pairs):
+                square = jnp.maximum(square_ref[:, blocks(k, 1)], tiny)
+                near = jnp.maximum(support - square * lax.rsqrt(square), 0.0)
+                link_ref[base, :, blocks(k, 1)] = (near * near * near).astype(bf16)
+            yield
+
+    def moments(tile, link_ref, base, parts, lane):
         total = None
-        for part, first in enumerate(firsts):
+        for first, pairs in parts:
             rows_all = []
-            for k in range(inner):
-                at, table = unpack(codes_ref[first + k], flux_rows, 8)
-                turn = turn_ref[table, :]
+            for k in range(first, first + pairs):
+                at, table = unpack(codes_ref[tile * slots + k], flux_rows, 8)
                 rows_all.append(
                     jnp.concatenate(
-                        [rows_ref[pl.ds(at, 32), :], rows_ref[pl.ds(at + 32, 8), :] * turn, zero],
+                        [rows_ref[pl.ds(at, 32), :], rows_ref[pl.ds(at + 32, 8), :] * turn_ref[table, :], zero],
                         axis=0,
                     ).astype(bf16)
                 )
             sums = lax.dot_general(
                 jnp.concatenate(rows_all, axis=1),
-                link_ref[base + part],
+                link_ref[base, :, blocks(lane + first, pairs)],
                 (((1,), (1,)), ((), ())),
                 preferred_element_type=f32,
             )
             total = sums if total is None else total + sums
+            yield
         sums_ref[pl.ds(pl.multiple_of(tile * flux_rows, 8), flux_rows), :] = total[0:flux_rows]
 
-    def pipeline(units, tiles_each, parts_each):
+    def pipeline(units, tiles_each, parts):
         last = units - 1
+        width = sum(pairs for first, pairs in parts)
 
         def tiles(unit):
             for k in range(tiles_each):
-                tile = tile_index(unit * tiles_each + k, count)
-                yield k, tile, [tile * slots + part * inner for part in range(parts_each)]
+                yield k * width, tile_index(unit * tiles_each + k, count)
 
         def stage_one(unit, square_ref):
-            for k, tile, firsts in tiles(jnp.minimum(unit, last)):
-                squares(tile, firsts, square_ref, k * parts_each)
+            for lane, tile in tiles(jnp.minimum(unit, last)):
+                yield from squares(tile, square_ref, parts, lane)
 
         def stage_two(unit, square_ref, link_ref):
-            weigh(square_ref, link_ref, unit // 2 * inner, tiles_each * parts_each)
+            for k in range(tiles_each):
+                yield from weigh(square_ref, link_ref, unit // 2, parts, k * width)
 
         def stage_three(unit, link_ref):
             unit = jnp.maximum(unit, 0)
-            for k, tile, firsts in tiles(unit):
-                moments(tile, firsts, link_ref, unit // 2 * inner + k * parts_each)
-
-        stage_one(0, square_a)
+            for lane, tile in tiles(unit):
+                yield from moments(tile, link_ref, unit // 2, parts, lane)
+
+        in_turns(stage_one(0, square_a))
 
         def body(step, carry):
             unit = step * 2
-            stage_one(unit + 1, square_b)
-            stage_two(unit, square_a, link_a)
-            stage_three(unit - 1, link_b)
-            stage_one(unit + 2, square_a)
-            stage_two(unit + 1, square_b, link_b)
-            stage_three(unit, link_a)
+            in_turns(
+                stage_one(unit + 1, square_b),
+                stage_two(unit, square_a, link_a),
+                stage_three(unit - 1, link_b),
+            )
+            in_turns(
+                stage_one(unit + 2, square_a),
+                stage_two(unit + 1, square_b, link_b),
+                stage_three(unit, link_a),
+            )
             return carry
 
         lax.fori_loop(0, units // 2, body, 0)
-        stage_three(last, link_b)
+        in_turns(stage_three(last, link_b))
 
     @pl.when(wall_ref[0] == 1)
     def _():
-        pipeline(count + 2 * rim, 1, slots // inner)
+        pipeline(count + 2 * rim, 1, wall_parts)
 
     @pl.when(wall_ref[0] == 0)
     def _():
-        pipeline((count + 2 * rim) // 2, 2, 1)
+        pipeline((count + 2 * rim) // 2, 2, inner_parts)
 
     def finish(chunk, carry):
         at = pl.multiple_of(chunk * 8, 8)
@@ -330,12 +349,12 @@
         def _():
             lax.fori_loop(0, span // 8, partial(prepare, strip, ref, ref_two), 0)
 
-    def moments(tile, firsts, link_ref, base):
+    def moments(tile, link_ref, base, parts, lane):
         total = None
-        for part, first in enumerate(firsts):
+        for first, pairs in parts:
             rows_all = []
-            for k in range(inner):
-                at, table = unpack(codes_ref[first + k], force_rows, 16)
+            for k in range(first, first + pairs):
+                at, table = unpack(codes_ref[tile * slots + k], force_rows, 16)
                 turn = turn_ref[table, :]
                 rows_all.append(
                     jnp.concatenate(
@@ -345,31 +364,36 @@
                 )
             sums = lax.dot_general(
                 jnp.concatenate(rows_all, axis=1),
-                link_ref[base + part],
+                link_ref[base, :, blocks(lane + first, pairs)],
                 (((1,), (1,)), ((), ())),
                 preferred_element_type=f32,
             )
             total = sums if total is None else total + sums
+            yield
         sums_ref[pl.ds(pl.multiple_of(tile * 16, 8), 16), :] = total[0:16] + total[16:32]
 
-    def sweep(steps, tiles_each, parts_each):
+    def sweep(steps, tiles_each, parts):
+        width = sum(pairs for first, pairs in parts)
+
         def body(step, carry):
-            for side, link_ref in enumerate((link_a, link_b)):
-                for k in range(tiles_each):
-                    tile = (step * 2 + side) * tiles_each + k
-                    firsts = [tile * slots + part * inner for part in range(parts_each)]
-                    moments(tile, firsts, link_ref, step * inner + k * parts_each)
+            in_turns(
+                *[
+                    moments((step * 2 + side) * tiles_each + k, link_ref, step, parts, k * width)
+                    for side, link_ref in enumerate((link_a, link_b))
+                    for k in range(tiles_each)
+                ]
+            )
             return carry
 
         lax.fori_loop(0, steps, body, 0)
 
     @pl.when(wall_ref[0] == 1)
     def _():
-        sweep(count // 2, 1, slots // inner)
+        sweep(count // 2, 1, wall_parts)
 
     @pl.when(wall_ref[0] == 0)
     def _():
-        sweep(count // 4, 2, 1)
+        sweep(count // 4, 2, inner_parts)
 
     def finish(chunk, carry):
         at = pl.multiple_of(chunk * 8, 8)
@@ -469,12 +493,12 @@
     up = lax.ppermute(mid, "trans", ring("trans", 1))
     down = lax.ppermute(mid, "trans", ring("trans", -1))
     listed = packed_list(ext[13, :, :slots].astype(jnp.int32), count)
-    groups = (count + 2 * rim) // 2 * (slots // inner)
+    units = (count + 2 * rim) // 2
     link_a, link_b, conc_ext, second = pl.pallas_call(
         partial(flux_kernel, count),
         out_shape=(
-            pltpu.VMEM((groups, lanes, inner * lanes), bf16),
-            pltpu.VMEM((groups, lanes, inner * lanes), bf16),
+            pltpu.VMEM((units, lanes, slots * lanes), bf16),
+            pltpu.VMEM((units, lanes, slots * lanes), bf16),
             jax.ShapeDtypeStruct((4, span, lanes), f32),
             jax.ShapeDtypeStruct((4, span, lanes), f32),
         ),
@@ -488,8 +512,8 @@
             pltpu.VMEM((15 * 8, lanes), f32),
             pltpu.VMEM((15 * 8, lanes), f32),
             pltpu.VMEM((15 * 8, lanes), f32),
-            pltpu.VMEM((inner, lanes, inner * lanes), f32),
-            pltpu.VMEM((inner, lanes, inner * lanes), f32),
+            pltpu.VMEM((lanes, slots * lanes), f32),
+            pltpu.VMEM((lanes, slots * lanes), f32),
         ],
         compiler_params=pltpu.CompilerParams(vmem_limit_bytes=vmem_bytes),
     )(listed, wall, params, ext, up, down)

time: 82.7 us -> 78.6 us (0.950)
  Pallas kernels: 46.2 us -> 42.1 us
    pallas_call x1, Pallas kernels: 30.9 us -> 26.7 us  [per_device(): pl.pallas_call(partial(flux_kernel, count), out_shape=(pltpu.VMEM((units,...]
where the time goes in v3:
time: 78.6 us; the launch traced here: 78.3 us
  Pallas kernels  42.1 us (54%)
  starting transfers between devices  27.4 us (35%)
  waiting for transfers between devices  4.43 us (6%)
  other arithmetic  2.56 us (3%)
  local copies, waits for them, and re-layouts  1.04 us (1%)
    pallas_call x1, Pallas kernels, per_device(): pl.pallas_call(partial(flux_kernel, count), out_shape=(pltpu.VMEM((units,...  26.7 us
    pallas_call x1, Pallas kernels, per_device(): pl.pallas_call(partial(force_kernel, count), out_shape=jax.ShapeDtypeStru...  13.5 us
    ppermute x1, starting transfers between devices, per_device(): other = lax.ppermute(other, 'stream', swaps('stream', 1))  10.8 us
    ppermute x1, starting transfers between devices, per_device(): first = lax.ppermute(first, 'stream', swaps('stream', 0))  8.81 us
    ppermute x1, starting transfers between devices, per_device(): down = lax.ppermute(mid, 'trans', ring('trans', -1))  3.94 us
    ppermute x1, waiting for transfers between devices, per_device(): up = lax.ppermute(mid, 'trans', ring('trans', 1))  2.04 us
    pallas_call x1, Pallas kernels, per_device(): pl.pallas_call(pack_kernel, out_shape=(jax.ShapeDtypeStruct((14, count, l...  1.91 us
  transfers between devices with their start and end apart: 6, of which 3 were waited for; matrix products, arithmetic and copies ran while one was open for 3% of the time, Pallas kernels for 0%

profile of v3, /device:TPU:97, one launch (start us, length us, event | category | flops | bytes accessed | tf_op | source)
XLA Modules:
  0.0 78.3 jit_solution(13220552628055812570)
XLA Ops:
  0.6 1.9 %shard_map.104 = (f32[14,64,128]{2,1,0:T(8,128)}, f32[14,4,128]{2,1,0:T(4,128)}, f32[14,4,128]{2,1,0:T(4,128)}) custom-call(s32[1]{0:T(128)} %bitcast.even_ref, f32[3,64,128]{2,1,0:T(8,128)} %bitcast.25, f32[3,64,128]{2,1,0:T(8,128)} %bitcast.26, f32[4,64,128]{2,1,0:T(8,128)} %bitcast.21, f32[64,128]{1,0:T(8,128)} %bitcast.27, f32[64,128]{1,0:T(8,128)} %bitcast.28, ...), custom_call_target="tpu_custom_call" | custom-call | tf_op jit(solution)/shard_map/pallas_call | solution.py:468
  2.6 8.8 %collective-permute-start = (f32[14,4,128]{2,1,0:T(4,128)}, f32[14,4,128]{2,1,0:T(4,128)S(1)}, u32[]{:S(2)}, u32[]{:S(2)}) collective-permute-start(f32[14,4,128]{2,1,0:T(4,128)} %get-tuple-element.10), channel_id=1, source_target_pairs={{0,8},{16,24},{32,40},{48,56},{64,72},{80,88},{96,104},{112,120},{... | collective-permute-start | bytes 86024 | tf_op jit(solution)/shard_map/ppermute | solution.py:487
  11.4 10.8 %collective-permute-start.1 = (f32[14,4,128]{2,1,0:T(4,128)}, f32[14,4,128]{2,1,0:T(4,128)S(1)}, u32[]{:S(2)}, u32[]{:S(2)}) collective-permute-start(f32[14,4,128]{2,1,0:T(4,128)} %get-tuple-element.11), channel_id=1, source_target_pairs={{8,16},{24,32},{40,48},{56,64},{72,80},{88,96},{104,112},{120,128}... | collective-permute-start | bytes 86024 | tf_op jit(solution)/shard_map/ppermute | solution.py:488
  22.2 0.7 convert_element_type.14
  22.8 0.1 pad_add_fusion.wall_ref
  22.9 0.7 pad_maximum_fusion.1.param_ref
  23.6 0.1 add.50
  23.7 0.1 add.51
  23.9 0.0 collective-permute-done
  23.9 1.1 %collective-permute-done.1 = f32[14,4,128]{2,1,0:T(4,128)S(1)} collective-permute-done((f32[14,4,128]{2,1,0:T(4,128)}, f32[14,4,128]{2,1,0:T(4,128)S(1)}, u32[]{:S(2)}, u32[]{:S(2)}) %collective-permute-start.1) | collective-permute-done | bytes 28704 | tf_op jit(solution)/shard_map/ppermute | solution.py:488
  25.0 1.1 %pad_maximum_fusion.ext_ref = f32[14,72,128]{2,1,0:T(8,128)S(1)} fusion(f32[14,4,128]{2,1,0:T(4,128)S(1)} %bitcast.23, f32[14,4,128]{2,1,0:T(4,128)S(1)} %bitcast.22, f32[14,64,128]{2,1,0:T(8,128)} %get-tuple-element.9), kind=kLoop, calls=%fused_computation | loop fusion | flops 258048 | bytes 1032192 | tf_op jit(solution)/shard_map/concatenate | solution.py:491
  26.1 3.9 %collective-permute-start.3 = (f32[9,72,128]{2,1,0:T(8,128)S(1)}, f32[9,72,128]{2,1,0:T(8,128)S(1)}, u32[]{:S(2)}, u32[]{:S(2)}) collective-permute-start(f32[9,72,128]{2,1,0:T(8,128)S(1)} %slice.13), channel_id=1, source_target_pairs={{1,0},{2,1},{3,2},{4,3},{5,4},{6,5},{7,6},{9,8},{10,9},{11,10},{12... | collective-permute-start | bytes 995336 | tf_op jit(solution)/shard_map/ppermute | solution.py:494
  30.0 1.3 %collective-permute-start.2 = (f32[9,72,128]{2,1,0:T(8,128)S(1)}, f32[9,72,128]{2,1,0:T(8,128)S(1)}, u32[]{:S(2)}, u32[]{:S(2)}) collective-permute-start(f32[9,72,128]{2,1,0:T(8,128)S(1)} %slice.13), channel_id=1, source_target_pairs={{0,1},{1,2},{2,3},{3,4},{4,5},{5,6},{6,7},{8,9},{9,10},{10,11},{11... | collective-permute-start | bytes 995336 | tf_op jit(solution)/shard_map/ppermute | solution.py:493
  31.3 0.1 convert_element_type.13
  31.5 0.0 collective-permute-done.3.down_ref
  31.5 2.0 %collective-permute-done.2.up_ref = f32[9,72,128]{2,1,0:T(8,128)S(1)} collective-permute-done((f32[9,72,128]{2,1,0:T(8,128)S(1)}, f32[9,72,128]{2,1,0:T(8,128)S(1)}, u32[]{:S(2)}, u32[]{:S(2)}) %collective-permute-start.2) | collective-permute-done | bytes 331808 | tf_op jit(solution)/shard_map/ppermute | solution.py:493
  33.5 26.7 %shard_map.105 = (bf16[34,128,1152]{2,1,0:T(8,128)(2,1)S(1)}, bf16[34,128,1152]{2,1,0:T(8,128)(2,1)S(1)}, f32[4,72,128]{2,1,0:T(8,128)S(1)}, f32[4,72,128]{2,1,0:T(8,128)S(1)}) custom-call(s32[648]{0:T(1024)S(1)} %fusion.3.codes_ref, s32[2]{0:T(128)S(1)} %pad_add_fusion.wall_ref, f32[8]{0:T(128)S(1)} %pad_maximum_fusion.1.param_ref, ...), custom_call_target="tpu_custom_call" | custom-call | tf_op jit(solution)/shard_map/pallas_call | solution.py:497
  60.3 1.3 %collective-permute-start.5 = (f32[4,72,128]{2,1,0:T(8,128)S(1)}, f32[4,72,128]{2,1,0:T(8,128)S(1)}, u32[]{:S(2)}, u32[]{:S(2)}) collective-permute-start(f32[4,72,128]{2,1,0:T(8,128)S(1)} %get-tuple-element.13.second_ref), channel_id=1, source_target_pairs={{1,0},{2,1},{3,2},{4,3},{5,4},{6,5},{7,6},{9,8},{10,9},{11,10},{12... | collective-permute-start | bytes 442376 | tf_op jit(solution)/shard_map/ppermute | solution.py:521
  61.6 1.3 %collective-permute-start.4 = (f32[4,72,128]{2,1,0:T(8,128)S(1)}, f32[4,72,128]{2,1,0:T(8,128)S(1)}, u32[]{:S(2)}, u32[]{:S(2)}) collective-permute-start(f32[4,72,128]{2,1,0:T(8,128)S(1)} %get-tuple-element.13.second_ref), channel_id=1, source_target_pairs={{0,1},{1,2},{2,3},{3,4},{4,5},{5,6},{6,7},{8,9},{9,10},{10,11},{11... | collective-permute-start | bytes 442376 | tf_op jit(solution)/shard_map/ppermute | solution.py:520
  62.9 0.7 slice_bitcast_fusion
  63.5 0.0 collective-permute-done.5.second_down_ref
  63.5 1.3 %collective-permute-done.4.second_up_ref = f32[4,72,128]{2,1,0:T(8,128)S(1)} collective-permute-done((f32[4,72,128]{2,1,0:T(8,128)S(1)}, f32[4,72,128]{2,1,0:T(8,128)S(1)}, u32[]{:S(2)}, u32[]{:S(2)}) %collective-permute-start.4) | collective-permute-done | bytes 147488 | tf_op jit(solution)/shard_map/ppermute | solution.py:520
  64.8 13.5 %shard_map.106 = f32[3,64,128]{2,1,0:T(8,128)} custom-call(s32[648]{0:T(1024)S(1)} %fusion.3.codes_ref, s32[2]{0:T(128)S(1)} %pad_add_fusion.wall_ref, f32[14,72,128]{2,1,0:T(8,128)S(1)} %pad_maximum_fusion.ext_ref, f32[9,72,128]{2,1,0:T(8,128)S(1)} %collective-permute-done.2.up_ref, f32[9,72,128]{2,1,0:T(8,128)S(1)} %collective-permute-done.3.down_ref, ...), custom_call_target="tpu_custom_call" | custom-call | tf_op jit(solution)/shard_map/pallas_call | solution.py:522
  (5 shorter events, 0.1 us)
Async XLA Ops:
  2.6 21.3 %collective-permute-start = (f32[14,4,128]{2,1,0:T(4,128)}, f32[14,4,128]{2,1,0:T(4,128)S(1)}, u32[]{:S(2)}, u32[]{:S(2)}) collective-permute-start(f32[14,4,128]{2,1,0:T(4,128)} %get-tuple-element.10), channel_id=1, source_target_pairs={{0,8},{16,24},{32,40},{48,56},{64,72},{80,88},{96,104},{112,120},{... | collective-permute-start | bytes 86024 | tf_op jit(solution)/shard_map/ppermute | solution.py:487
  11.4 13.6 %collective-permute-start.1 = (f32[14,4,128]{2,1,0:T(4,128)}, f32[14,4,128]{2,1,0:T(4,128)S(1)}, u32[]{:S(2)}, u32[]{:S(2)}) collective-permute-start(f32[14,4,128]{2,1,0:T(4,128)} %get-tuple-element.11), channel_id=1, source_target_pairs={{8,16},{24,32},{40,48},{56,64},{72,80},{88,96},{104,112},{120,128}... | collective-permute-start | bytes 86024 | tf_op jit(solution)/shard_map/ppermute | solution.py:488
  26.1 5.4 %collective-permute-start.3 = (f32[9,72,128]{2,1,0:T(8,128)S(1)}, f32[9,72,128]{2,1,0:T(8,128)S(1)}, u32[]{:S(2)}, u32[]{:S(2)}) collective-permute-start(f32[9,72,128]{2,1,0:T(8,128)S(1)} %slice.13), channel_id=1, source_target_pairs={{1,0},{2,1},{3,2},{4,3},{5,4},{6,5},{7,6},{9,8},{10,9},{11,10},{12... | collective-permute-start | bytes 995336 | tf_op jit(solution)/shard_map/ppermute | solution.py:494
  30.0 3.5 %collective-permute-start.2 = (f32[9,72,128]{2,1,0:T(8,128)S(1)}, f32[9,72,128]{2,1,0:T(8,128)S(1)}, u32[]{:S(2)}, u32[]{:S(2)}) collective-permute-start(f32[9,72,128]{2,1,0:T(8,128)S(1)} %slice.13), channel_id=1, source_target_pairs={{0,1},{1,2},{2,3},{3,4},{4,5},{5,6},{6,7},{8,9},{9,10},{10,11},{11... | collective-permute-start | bytes 995336 | tf_op jit(solution)/shard_map/ppermute | solution.py:493
  60.3 3.3 %collective-permute-start.5 = (f32[4,72,128]{2,1,0:T(8,128)S(1)}, f32[4,72,128]{2,1,0:T(8,128)S(1)}, u32[]{:S(2)}, u32[]{:S(2)}) collective-permute-start(f32[4,72,128]{2,1,0:T(8,128)S(1)} %get-tuple-element.13.second_ref), channel_id=1, source_target_pairs={{1,0},{2,1},{3,2},{4,3},{5,4},{6,5},{7,6},{9,8},{10,9},{11,10},{12... | collective-permute-start | bytes 442376 | tf_op jit(solution)/shard_map/ppermute | solution.py:521
  61.6 3.3 %collective-permute-start.4 = (f32[4,72,128]{2,1,0:T(8,128)S(1)}, f32[4,72,128]{2,1,0:T(8,128)S(1)}, u32[]{:S(2)}, u32[]{:S(2)}) collective-permute-start(f32[4,72,128]{2,1,0:T(8,128)S(1)} %get-tuple-element.13.second_ref), channel_id=1, source_target_pairs={{0,1},{1,2},{2,3},{3,4},{4,5},{5,6},{6,7},{8,9},{9,10},{10,11},{11... | collective-permute-start | bytes 442376 | tf_op jit(solution)/shard_map/ppermute | solution.py:520

commit v4 on v3

--- a/solution.py
+++ b/solution.py
@@ -85,18 +85,14 @@
         stages = [stage for stage in stages if next(stage, stages) is None]
 
 
-def used(wall_ref, strip):
-    return (wall_ref[0] == 0) | (wall_ref[1] == strip - 1)
-
-
 def flux_kernel(
     count,
     codes_ref,
     wall_ref,
     param_ref,
     ext_ref,
-    up_ref,
-    down_ref,
+    mate_ref,
+    next_ref,
     link_a,
     link_b,
     conc_ref,
@@ -156,11 +152,11 @@
         return carry
 
     lax.fori_loop(0, span // 8, partial(prepare, 1, ext_ref, True), 0)
-    for strip, ref in ((0, up_ref), (2, down_ref)):
-
-        @pl.when(used(wall_ref, strip))
-        def _():
-            lax.fori_loop(0, span // 8, partial(prepare, strip, ref, False), 0)
+    lax.fori_loop(0, span // 8, partial(prepare, wall_ref[1], mate_ref, False), 0)
+
+    @pl.when(wall_ref[0] == 0)
+    def _():
+        lax.fori_loop(0, span // 8, partial(prepare, 2 - wall_ref[1], next_ref, False), 0)
 
     def squares(tile, square_ref, parts, lane):
         own = own_ref[pl.ds(pl.multiple_of(tile * own_rows, 8), own_rows), :].T.astype(bf16)
@@ -303,11 +299,11 @@
     codes_ref,
     wall_ref,
     ext_ref,
-    up_ref,
-    down_ref,
+    mate_ref,
+    next_ref,
     second_ref,
-    second_up_ref,
-    second_down_ref,
+    second_mate_ref,
+    second_next_ref,
     link_a,
     link_b,
     out_ref,
@@ -343,11 +339,11 @@
         return carry
 
     lax.fori_loop(0, span // 8, partial(prepare, 1, ext_ref, second_ref), 0)
-    for strip, ref, ref_two in ((0, up_ref, second_up_ref), (2, down_ref, second_down_ref)):
-
-        @pl.when(used(wall_ref, strip))
-        def _():
-            lax.fori_loop(0, span // 8, partial(prepare, strip, ref, ref_two), 0)
+    lax.fori_loop(0, span // 8, partial(prepare, wall_ref[1], mate_ref, second_mate_ref), 0)
+
+    @pl.when(wall_ref[0] == 0)
+    def _():
+        lax.fori_loop(0, span // 8, partial(prepare, 2 - wall_ref[1], next_ref, second_next_ref), 0)
 
     def moments(tile, link_ref, base, parts, lane):
         total = None
@@ -446,13 +442,9 @@
 
 def swaps(axis, start):
     size = lax.axis_size(axis)
-    pairs = [(i, (i + 1) % size) for i in range(start, size, 2)]
+    stop = size - start if axis == "trans" else size
+    pairs = [(i, (i + 1) % size) for i in range(start, stop, 2)]
     return pairs + [(j, i) for i, j in pairs]
-
-
-def ring(axis, step):
-    size = lax.axis_size(axis)
-    return [(i, i + step) for i in range(size) if 0 <= i + step < size]
 
 
 def per_device(offsets, velocity, conc, potential, mass, density, diffusivity, valence, pair_codes):
@@ -460,7 +452,7 @@
     span = count + 2 * halo
     place = lax.axis_index("trans")
     last = lax.axis_size("trans") - 1
-    wall = jnp.stack([(place == 0) | (place == last), jnp.where(place == 0, 1, -1)]).astype(jnp.int32)
+    wall = jnp.stack([(place == 0) | (place == last), 2 - place % 2 * 2]).astype(jnp.int32)
     params = jnp.concatenate([diffusivity, valence.astype(f32)])
     smem = pl.BlockSpec(memory_space=pltpu.SMEM)
     vmem = pl.BlockSpec(memory_space=pltpu.VMEM)
@@ -490,8 +482,9 @@
     left = jnp.where(even, other, first)
     ext = jnp.concatenate([own, right, left], axis=1)
     mid = ext[0:9]
-    up = lax.ppermute(mid, "trans", ring("trans", 1))
-    down = lax.ppermute(mid, "trans", ring("trans", -1))
+    mate = lax.ppermute(mid, "trans", swaps("trans", 0))
+    mid, mate = lax.optimization_barrier((mid, mate))
+    after = lax.ppermute(mid, "trans", swaps("trans", 1))
     listed = packed_list(ext[13, :, :slots].astype(jnp.int32), count)
     units = (count + 2 * rim) // 2
     link_a, link_b, conc_ext, second = pl.pallas_call(
@@ -516,9 +509,10 @@
             pltpu.VMEM((lanes, slots * lanes), f32),
         ],
         compiler_params=pltpu.CompilerParams(vmem_limit_bytes=vmem_bytes),
-    )(listed, wall, params, ext, up, down)
-    second_up = lax.ppermute(second, "trans", ring("trans", 1))
-    second_down = lax.ppermute(second, "trans", ring("trans", -1))
+    )(listed, wall, params, ext, mate, after)
+    second_mate = lax.ppermute(second, "trans", swaps("trans", 0))
+    second, second_mate = lax.optimization_barrier((second, second_mate))
+    second_after = lax.ppermute(second, "trans", swaps("trans", 1))
     velocity_new = pl.pallas_call(
         partial(force_kernel, count),
         out_shape=jax.ShapeDtypeStruct((3, count, lanes), f32),
@@ -534,11 +528,11 @@
         listed,
         wall,
         ext,
-        up,
-        down,
+        mate,
+        after,
         second,
-        second_up,
-        second_down,
+        second_mate,
+        second_after,
         pltpu.with_memory_space_constraint(link_a, pltpu.VMEM),
         pltpu.with_memory_space_constraint(link_b, pltpu.VMEM),
     )

time: 78.6 us -> 78.5 us (level)
  the two profiles are of different devices: /device:TPU:97 before, /device:TPU:1 now
where the time goes in v4:
time: 78.5 us; the launch traced here: 78.2 us
  starting transfers between devices  40 us (51%)
  Pallas kernels  21.9 us (28%)
  waiting for transfers between devices  12 us (15%)
  other arithmetic  2.57 us (3%)
  local copies, waits for them, and re-layouts  1.05 us (1%)
    ppermute x1, starting transfers between devices, per_device(): other = lax.ppermute(other, 'stream', swaps('stream', 1))  13.5 us
    pallas_call x1, Pallas kernels, per_device(): pl.pallas_call(partial(flux_kernel, count), out_shape=(pltpu.VMEM((units,...  12.3 us
    ppermute x1, starting transfers between devices, per_device(): first = lax.ppermute(first, 'stream', swaps('stream', 0))  9.63 us
    ppermute x1, starting transfers between devices, per_device(): second_mate = lax.ppermute(second, 'trans', swaps('trans', 0))  9.14 us
    pallas_call x1, Pallas kernels, per_device(): pl.pallas_call(partial(force_kernel, count), out_shape=jax.ShapeDtypeStru...  7.67 us
    ppermute x1, waiting for transfers between devices, per_device(): after = lax.ppermute(mid, 'trans', swaps('trans', 1))  5.3 us
    ppermute x1, waiting for transfers between devices, per_device(): second_after = lax.ppermute(second, 'trans', swaps('trans', 1))  3.87 us
    ppermute x1, starting transfers between devices, per_device(): after = lax.ppermute(mid, 'trans', swaps('trans', 1))  2.93 us
  transfers between devices with their start and end apart: 6, of which 5 were waited for; matrix products, arithmetic and copies ran while one was open for 3% of the time, Pallas kernels for 0%

profile of v4, /device:TPU:1, one launch (start us, length us, event | category | flops | bytes accessed | tf_op | source)
XLA Modules:
  0.0 78.2 jit_solution(8313213118671790403)
XLA Ops:
  0.6 1.9 %shard_map.104 = (f32[14,64,128]{2,1,0:T(8,128)}, f32[14,4,128]{2,1,0:T(4,128)}, f32[14,4,128]{2,1,0:T(4,128)}) custom-call(s32[1]{0:T(128)} %bitcast.even_ref, f32[3,64,128]{2,1,0:T(8,128)} %bitcast.25, f32[3,64,128]{2,1,0:T(8,128)} %bitcast.26, f32[4,64,128]{2,1,0:T(8,128)} %bitcast.21, f32[64,128]{1,0:T(8,128)} %bitcast.27, f32[64,128]{1,0:T(8,128)} %bitcast.28, ...), custom_call_target="tpu_custom_call" | custom-call | tf_op jit(solution)/shard_map/pallas_call | solution.py:460
  2.6 9.6 %collective-permute-start = (f32[14,4,128]{2,1,0:T(4,128)}, f32[14,4,128]{2,1,0:T(4,128)S(1)}, u32[]{:S(2)}, u32[]{:S(2)}) collective-permute-start(f32[14,4,128]{2,1,0:T(4,128)} %get-tuple-element.14), channel_id=1, source_target_pairs={{0,8},{16,24},{32,40},{48,56},{64,72},{80,88},{96,104},{112,120},{... | collective-permute-start | bytes 86024 | tf_op jit(solution)/shard_map/ppermute | solution.py:479
  12.2 13.5 %collective-permute-start.1 = (f32[14,4,128]{2,1,0:T(4,128)}, f32[14,4,128]{2,1,0:T(4,128)S(1)}, u32[]{:S(2)}, u32[]{:S(2)}) collective-permute-start(f32[14,4,128]{2,1,0:T(4,128)} %get-tuple-element.15), channel_id=1, source_target_pairs={{8,16},{24,32},{40,48},{56,64},{72,80},{88,96},{104,112},{120,128}... | collective-permute-start | bytes 86024 | tf_op jit(solution)/shard_map/ppermute | solution.py:480
  25.7 0.7 convert_element_type.14
  26.3 0.0 collective-permute-done
  26.3 1.6 %collective-permute-done.1 = f32[14,4,128]{2,1,0:T(4,128)S(1)} collective-permute-done((f32[14,4,128]{2,1,0:T(4,128)}, f32[14,4,128]{2,1,0:T(4,128)S(1)}, u32[]{:S(2)}, u32[]{:S(2)}) %collective-permute-start.1) | collective-permute-done | bytes 28704 | tf_op jit(solution)/shard_map/ppermute | solution.py:480
  28.0 1.1 %pad_maximum_fusion.ext_ref = f32[14,72,128]{2,1,0:T(8,128)S(1)} fusion(f32[14,4,128]{2,1,0:T(4,128)S(1)} %bitcast.23, f32[14,4,128]{2,1,0:T(4,128)S(1)} %bitcast.22, f32[14,64,128]{2,1,0:T(8,128)} %get-tuple-element.13), kind=kLoop, calls=%fused_computation | loop fusion | flops 258048 | bytes 1032192 | tf_op jit(solution)/shard_map/concatenate | solution.py:483
  29.1 2.9 %collective-permute-start.2 = (f32[9,72,128]{2,1,0:T(8,128)S(1)}, f32[9,72,128]{2,1,0:T(8,128)S(1)}, u32[]{:S(2)}, u32[]{:S(2)}) collective-permute-start(f32[9,72,128]{2,1,0:T(8,128)S(1)} %slice.13), channel_id=1, source_target_pairs={{0,1},{2,3},{4,5},{6,7},{1,0},{3,2},{5,4},{7,6},{8,9},{10,11},{12,... | collective-permute-start | bytes 995336 | tf_op jit(solution)/shard_map/ppermute | solution.py:485
  32.0 0.1 add.53
  32.1 0.1 add.54
  32.2 0.1 pad_add_fusion.wall_ref
  32.3 0.7 pad_maximum_fusion.1.param_ref
  33.0 0.2 collective-permute-done.2.mate_ref
  33.2 2.9 %collective-permute-start.3 = (f32[9,72,128]{2,1,0:T(8,128)S(1)}, f32[9,72,128]{2,1,0:T(8,128)S(1)}, u32[]{:S(2)}, u32[]{:S(2)}) collective-permute-start(f32[9,72,128]{2,1,0:T(8,128)S(1)} %slice.13), channel_id=1, source_target_pairs={{1,2},{3,4},{5,6},{2,1},{4,3},{6,5},{9,10},{11,12},{13,14},{10,9},... | collective-permute-start | bytes 995336 | tf_op jit(solution)/shard_map/ppermute | solution.py:487
  36.2 0.1 convert_element_type.13
  36.3 5.3 %collective-permute-done.3.next_ref = f32[9,72,128]{2,1,0:T(8,128)S(1)} collective-permute-done((f32[9,72,128]{2,1,0:T(8,128)S(1)}, f32[9,72,128]{2,1,0:T(8,128)S(1)}, u32[]{:S(2)}, u32[]{:S(2)}) %collective-permute-start.3) | collective-permute-done | bytes 331808 | tf_op jit(solution)/shard_map/ppermute | solution.py:487
  41.6 12.3 %shard_map.105 = (bf16[34,128,1152]{2,1,0:T(8,128)(2,1)S(1)}, bf16[34,128,1152]{2,1,0:T(8,128)(2,1)S(1)}, f32[4,72,128]{2,1,0:T(8,128)S(1)}, f32[4,72,128]{2,1,0:T(8,128)S(1)}) custom-call(s32[648]{0:T(1024)S(1)} %fusion.3.codes_ref, s32[2]{0:T(128)S(1)} %pad_add_fusion.wall_ref, f32[8]{0:T(128)S(1)} %pad_maximum_fusion.1.param_ref, ...), custom_call_target="tpu_custom_call" | custom-call | tf_op jit(solution)/shard_map/pallas_call | solution.py:490
  54.0 9.1 %collective-permute-start.4 = (f32[4,72,128]{2,1,0:T(8,128)S(1)}, f32[4,72,128]{2,1,0:T(8,128)S(1)}, u32[]{:S(2)}, u32[]{:S(2)}) collective-permute-start(f32[4,72,128]{2,1,0:T(8,128)S(1)} %get-tuple-element.20.second_ref), channel_id=1, source_target_pairs={{0,1},{2,3},{4,5},{6,7},{1,0},{3,2},{5,4},{7,6},{8,9},{10,11},{12,... | collective-permute-start | bytes 442376 | tf_op jit(solution)/shard_map/ppermute | solution.py:513
  63.1 1.0 %collective-permute-done.4.second_mate_ref = f32[4,72,128]{2,1,0:T(8,128)S(1)} collective-permute-done((f32[4,72,128]{2,1,0:T(8,128)S(1)}, f32[4,72,128]{2,1,0:T(8,128)S(1)}, u32[]{:S(2)}, u32[]{:S(2)}) %collective-permute-start.4) | collective-permute-done | bytes 147488 | tf_op jit(solution)/shard_map/ppermute | solution.py:513
  64.1 1.9 %collective-permute-start.5 = (f32[4,72,128]{2,1,0:T(8,128)S(1)}, f32[4,72,128]{2,1,0:T(8,128)S(1)}, u32[]{:S(2)}, u32[]{:S(2)}) collective-permute-start(f32[4,72,128]{2,1,0:T(8,128)S(1)} %get-tuple-element.20.second_ref), channel_id=1, source_target_pairs={{1,2},{3,4},{5,6},{2,1},{4,3},{6,5},{9,10},{11,12},{13,14},{10,9},... | collective-permute-start | bytes 442376 | tf_op jit(solution)/shard_map/ppermute | solution.py:515
  66.0 0.7 slice_bitcast_fusion
  66.7 3.9 %collective-permute-done.5.second_next_ref = f32[4,72,128]{2,1,0:T(8,128)S(1)} collective-permute-done((f32[4,72,128]{2,1,0:T(8,128)S(1)}, f32[4,72,128]{2,1,0:T(8,128)S(1)}, u32[]{:S(2)}, u32[]{:S(2)}) %collective-permute-start.5) | collective-permute-done | bytes 147488 | tf_op jit(solution)/shard_map/ppermute | solution.py:515
  70.5 7.7 %shard_map.106 = f32[3,64,128]{2,1,0:T(8,128)} custom-call(s32[648]{0:T(1024)S(1)} %fusion.3.codes_ref, s32[2]{0:T(128)S(1)} %pad_add_fusion.wall_ref, f32[14,72,128]{2,1,0:T(8,128)S(1)} %pad_maximum_fusion.ext_ref, f32[9,72,128]{2,1,0:T(8,128)S(1)} %collective-permute-done.2.mate_ref, f32[9,72,128]{2,1,0:T(8,128)S(1)} %collective-permute-done.3.next_ref, ...), custom_call_target="tpu_custom_call" | custom-call | tf_op jit(solution)/shard_map/pallas_call | solution.py:516
  (5 shorter events, 0.1 us)
Async XLA Ops:
  2.6 23.8 %collective-permute-start = (f32[14,4,128]{2,1,0:T(4,128)}, f32[14,4,128]{2,1,0:T(4,128)S(1)}, u32[]{:S(2)}, u32[]{:S(2)}) collective-permute-start(f32[14,4,128]{2,1,0:T(4,128)} %get-tuple-element.14), channel_id=1, source_target_pairs={{0,8},{16,24},{32,40},{48,56},{64,72},{80,88},{96,104},{112,120},{... | collective-permute-start | bytes 86024 | tf_op jit(solution)/shard_map/ppermute | solution.py:479
  12.2 15.8 %collective-permute-start.1 = (f32[14,4,128]{2,1,0:T(4,128)}, f32[14,4,128]{2,1,0:T(4,128)S(1)}, u32[]{:S(2)}, u32[]{:S(2)}) collective-permute-start(f32[14,4,128]{2,1,0:T(4,128)} %get-tuple-element.15), channel_id=1, source_target_pairs={{8,16},{24,32},{40,48},{56,64},{72,80},{88,96},{104,112},{120,128}... | collective-permute-start | bytes 86024 | tf_op jit(solution)/shard_map/ppermute | solution.py:480
  29.1 4.2 %collective-permute-start.2 = (f32[9,72,128]{2,1,0:T(8,128)S(1)}, f32[9,72,128]{2,1,0:T(8,128)S(1)}, u32[]{:S(2)}, u32[]{:S(2)}) collective-permute-start(f32[9,72,128]{2,1,0:T(8,128)S(1)} %slice.13), channel_id=1, source_target_pairs={{0,1},{2,3},{4,5},{6,7},{1,0},{3,2},{5,4},{7,6},{8,9},{10,11},{12,... | collective-permute-start | bytes 995336 | tf_op jit(solution)/shard_map/ppermute | solution.py:485
  33.2 8.4 %collective-permute-start.3 = (f32[9,72,128]{2,1,0:T(8,128)S(1)}, f32[9,72,128]{2,1,0:T(8,128)S(1)}, u32[]{:S(2)}, u32[]{:S(2)}) collective-permute-start(f32[9,72,128]{2,1,0:T(8,128)S(1)} %slice.13), channel_id=1, source_target_pairs={{1,2},{3,4},{5,6},{2,1},{4,3},{6,5},{9,10},{11,12},{13,14},{10,9},... | collective-permute-start | bytes 995336 | tf_op jit(solution)/shard_map/ppermute | solution.py:487
  54.0 10.1 %collective-permute-start.4 = (f32[4,72,128]{2,1,0:T(8,128)S(1)}, f32[4,72,128]{2,1,0:T(8,128)S(1)}, u32[]{:S(2)}, u32[]{:S(2)}) collective-permute-start(f32[4,72,128]{2,1,0:T(8,128)S(1)} %get-tuple-element.20.second_ref), channel_id=1, source_target_pairs={{0,1},{2,3},{4,5},{6,7},{1,0},{3,2},{5,4},{7,6},{8,9},{10,11},{12,... | collective-permute-start | bytes 442376 | tf_op jit(solution)/shard_map/ppermute | solution.py:513
  64.1 6.5 %collective-permute-start.5 = (f32[4,72,128]{2,1,0:T(8,128)S(1)}, f32[4,72,128]{2,1,0:T(8,128)S(1)}, u32[]{:S(2)}, u32[]{:S(2)}) collective-permute-start(f32[4,72,128]{2,1,0:T(8,128)S(1)} %get-tuple-element.20.second_ref), channel_id=1, source_target_pairs={{1,2},{3,4},{5,6},{2,1},{4,3},{6,5},{9,10},{11,12},{13,14},{10,9},... | collective-permute-start | bytes 442376 | tf_op jit(solution)/shard_map/ppermute | solution.py:515

commit v5 on v4

--- a/solution.py
+++ b/solution.py
@@ -511,7 +511,6 @@
         compiler_params=pltpu.CompilerParams(vmem_limit_bytes=vmem_bytes),
     )(listed, wall, params, ext, mate, after)
     second_mate = lax.ppermute(second, "trans", swaps("trans", 0))
-    second, second_mate = lax.optimization_barrier((second, second_mate))
     second_after = lax.ppermute(second, "trans", swaps("trans", 1))
     velocity_new = pl.pallas_call(
         partial(force_kernel, count),

time: 78.5 us -> 76.4 us (0.973)
  the two profiles are of different devices: /device:TPU:1 before, /device:TPU:97 now
where the time goes in v5:
time: 76.4 us; the launch traced here: 76.1 us
  Pallas kernels  41.9 us (55%)
  starting transfers between devices  26.8 us (35%)
  waiting for transfers between devices  3.01 us (4%)
  other arithmetic  2.57 us (3%)
  local copies, waits for them, and re-layouts  1.05 us (1%)
  between operations  0.77 us (1%)
    pallas_call x1, Pallas kernels, per_device(): pl.pallas_call(partial(flux_kernel, count), out_shape=(pltpu.VMEM((units,...  26.7 us
    pallas_call x1, Pallas kernels, per_device(): pl.pallas_call(partial(force_kernel, count), out_shape=jax.ShapeDtypeStru...  13.3 us
    ppermute x1, starting transfers between devices, per_device(): other = lax.ppermute(other, 'stream', swaps('stream', 1))  10.8 us
    ppermute x1, starting transfers between devices, per_device(): first = lax.ppermute(first, 'stream', swaps('stream', 0))  8.81 us
    ppermute x1, starting transfers between devices, per_device(): mate = lax.ppermute(mid, 'trans', swaps('trans', 0))  3.93 us
    ppermute x1, waiting for transfers between devices, per_device(): other = lax.ppermute(other, 'stream', swaps('stream', 1))  2.13 us
    ppermute x1, starting transfers between devices, per_device(): second_mate = lax.ppermute(second, 'trans', swaps('trans', 0))  1.92 us
    pallas_call x1, Pallas kernels, per_device(): pl.pallas_call(pack_kernel, out_shape=(jax.ShapeDtypeStruct((14, count, l...  1.91 us
  transfers between devices with their start and end apart: 6, of which 3 were waited for; matrix products, arithmetic and copies ran while one was open for 3% of the time, Pallas kernels for 0%

profile of v5, /device:TPU:97, one launch (start us, length us, event | category | flops | bytes accessed | tf_op | source)
XLA Modules:
  0.0 76.1 jit_solution(459500450392477706)
XLA Ops:
  0.6 1.9 %shard_map.104 = (f32[14,64,128]{2,1,0:T(8,128)}, f32[14,4,128]{2,1,0:T(4,128)}, f32[14,4,128]{2,1,0:T(4,128)}) custom-call(s32[1]{0:T(128)} %bitcast.even_ref, f32[3,64,128]{2,1,0:T(8,128)} %bitcast.25, f32[3,64,128]{2,1,0:T(8,128)} %bitcast.26, f32[4,64,128]{2,1,0:T(8,128)} %bitcast.21, f32[64,128]{1,0:T(8,128)} %bitcast.27, f32[64,128]{1,0:T(8,128)} %bitcast.28, ...), custom_call_target="tpu_custom_call" | custom-call | tf_op jit(solution)/shard_map/pallas_call | solution.py:460
  2.6 8.8 %collective-permute-start = (f32[14,4,128]{2,1,0:T(4,128)}, f32[14,4,128]{2,1,0:T(4,128)S(1)}, u32[]{:S(2)}, u32[]{:S(2)}) collective-permute-start(f32[14,4,128]{2,1,0:T(4,128)} %get-tuple-element.12), channel_id=1, source_target_pairs={{0,8},{16,24},{32,40},{48,56},{64,72},{80,88},{96,104},{112,120},{... | collective-permute-start | bytes 86024 | tf_op jit(solution)/shard_map/ppermute | solution.py:479
  11.4 10.8 %collective-permute-start.1 = (f32[14,4,128]{2,1,0:T(4,128)}, f32[14,4,128]{2,1,0:T(4,128)S(1)}, u32[]{:S(2)}, u32[]{:S(2)}) collective-permute-start(f32[14,4,128]{2,1,0:T(4,128)} %get-tuple-element.13), channel_id=1, source_target_pairs={{8,16},{24,32},{40,48},{56,64},{72,80},{88,96},{104,112},{120,128}... | collective-permute-start | bytes 86024 | tf_op jit(solution)/shard_map/ppermute | solution.py:480
  22.2 0.7 convert_element_type.14
  22.8 0.0 collective-permute-done
  22.8 2.1 %collective-permute-done.1 = f32[14,4,128]{2,1,0:T(4,128)S(1)} collective-permute-done((f32[14,4,128]{2,1,0:T(4,128)}, f32[14,4,128]{2,1,0:T(4,128)S(1)}, u32[]{:S(2)}, u32[]{:S(2)}) %collective-permute-start.1) | collective-permute-done | bytes 28704 | tf_op jit(solution)/shard_map/ppermute | solution.py:480
  25.0 1.1 %pad_maximum_fusion.ext_ref = f32[14,72,128]{2,1,0:T(8,128)S(1)} fusion(f32[14,4,128]{2,1,0:T(4,128)S(1)} %bitcast.23, f32[14,4,128]{2,1,0:T(4,128)S(1)} %bitcast.22, f32[14,64,128]{2,1,0:T(8,128)} %get-tuple-element.11), kind=kLoop, calls=%fused_computation | loop fusion | flops 258048 | bytes 1032192 | tf_op jit(solution)/shard_map/concatenate | solution.py:483
  26.1 3.9 %collective-permute-start.2 = (f32[9,72,128]{2,1,0:T(8,128)S(1)}, f32[9,72,128]{2,1,0:T(8,128)S(1)}, u32[]{:S(2)}, u32[]{:S(2)}) collective-permute-start(f32[9,72,128]{2,1,0:T(8,128)S(1)} %slice.13), channel_id=1, source_target_pairs={{0,1},{2,3},{4,5},{6,7},{1,0},{3,2},{5,4},{7,6},{8,9},{10,11},{12,... | collective-permute-start | bytes 995336 | tf_op jit(solution)/shard_map/ppermute | solution.py:485
  30.0 0.1 add.53
  30.1 0.1 add.54
  30.2 0.1 pad_add_fusion.wall_ref
  30.3 0.7 pad_maximum_fusion.1.param_ref
  31.0 0.2 collective-permute-done.2.mate_ref
  31.2 0.7 collective-permute-start.3
  31.9 0.1 convert_element_type.13
  32.1 0.0 collective-permute-done.3.next_ref
  32.1 26.7 %shard_map.105 = (bf16[34,128,1152]{2,1,0:T(8,128)(2,1)S(1)}, bf16[34,128,1152]{2,1,0:T(8,128)(2,1)S(1)}, f32[4,72,128]{2,1,0:T(8,128)S(1)}, f32[4,72,128]{2,1,0:T(8,128)S(1)}) custom-call(s32[648]{0:T(1024)S(1)} %fusion.3.codes_ref, s32[2]{0:T(128)S(1)} %pad_add_fusion.wall_ref, f32[8]{0:T(128)S(1)} %pad_maximum_fusion.1.param_ref, ...), custom_call_target="tpu_custom_call" | custom-call | tf_op jit(solution)/shard_map/pallas_call | solution.py:490
  58.8 0.7 collective-permute-start.5
  59.5 1.9 %collective-permute-start.4 = (f32[4,72,128]{2,1,0:T(8,128)S(1)}, f32[4,72,128]{2,1,0:T(8,128)S(1)}, u32[]{:S(2)}, u32[]{:S(2)}) collective-permute-start(f32[4,72,128]{2,1,0:T(8,128)S(1)} %get-tuple-element.17.second_ref), channel_id=1, source_target_pairs={{0,1},{2,3},{4,5},{6,7},{1,0},{3,2},{5,4},{7,6},{8,9},{10,11},{12,... | collective-permute-start | bytes 442376 | tf_op jit(solution)/shard_map/ppermute | solution.py:513
  61.4 0.7 slice_bitcast_fusion
  62.1 0.0 collective-permute-done.5.second_next_ref
  62.1 0.7 collective-permute-done.4.second_mate_ref
  62.8 13.3 %shard_map.106 = f32[3,64,128]{2,1,0:T(8,128)} custom-call(s32[648]{0:T(1024)S(1)} %fusion.3.codes_ref, s32[2]{0:T(128)S(1)} %pad_add_fusion.wall_ref, f32[14,72,128]{2,1,0:T(8,128)S(1)} %pad_maximum_fusion.ext_ref, f32[9,72,128]{2,1,0:T(8,128)S(1)} %collective-permute-done.2.mate_ref, f32[9,72,128]{2,1,0:T(8,128)S(1)} %collective-permute-done.3.next_ref, ...), custom_call_target="tpu_custom_call" | custom-call | tf_op jit(solution)/shard_map/pallas_call | solution.py:515
  (5 shorter events, 0.1 us)
Async XLA Ops:
  2.6 20.3 %collective-permute-start = (f32[14,4,128]{2,1,0:T(4,128)}, f32[14,4,128]{2,1,0:T(4,128)S(1)}, u32[]{:S(2)}, u32[]{:S(2)}) collective-permute-start(f32[14,4,128]{2,1,0:T(4,128)} %get-tuple-element.12), channel_id=1, source_target_pairs={{0,8},{16,24},{32,40},{48,56},{64,72},{80,88},{96,104},{112,120},{... | collective-permute-start | bytes 86024 | tf_op jit(solution)/shard_map/ppermute | solution.py:479
  11.4 13.6 %collective-permute-start.1 = (f32[14,4,128]{2,1,0:T(4,128)}, f32[14,4,128]{2,1,0:T(4,128)S(1)}, u32[]{:S(2)}, u32[]{:S(2)}) collective-permute-start(f32[14,4,128]{2,1,0:T(4,128)} %get-tuple-element.13), channel_id=1, source_target_pairs={{8,16},{24,32},{40,48},{56,64},{72,80},{88,96},{104,112},{120,128}... | collective-permute-start | bytes 86024 | tf_op jit(solution)/shard_map/ppermute | solution.py:480
  26.1 5.2 %collective-permute-start.2 = (f32[9,72,128]{2,1,0:T(8,128)S(1)}, f32[9,72,128]{2,1,0:T(8,128)S(1)}, u32[]{:S(2)}, u32[]{:S(2)}) collective-permute-start(f32[9,72,128]{2,1,0:T(8,128)S(1)} %slice.13), channel_id=1, source_target_pairs={{0,1},{2,3},{4,5},{6,7},{1,0},{3,2},{5,4},{7,6},{8,9},{10,11},{12,... | collective-permute-start | bytes 995336 | tf_op jit(solution)/shard_map/ppermute | solution.py:485
  31.2 0.9 %collective-permute-start.3 = (f32[9,72,128]{2,1,0:T(8,128)S(1)}, f32[9,72,128]{2,1,0:T(8,128)S(1)}, u32[]{:S(2)}, u32[]{:S(2)}) collective-permute-start(f32[9,72,128]{2,1,0:T(8,128)S(1)} %slice.13), channel_id=1, source_target_pairs={{1,2},{3,4},{5,6},{2,1},{4,3},{6,5},{9,10},{11,12},{13,14},{10,9},... | collective-permute-start | bytes 995336 | tf_op jit(solution)/shard_map/ppermute | solution.py:487
  58.8 3.3 %collective-permute-start.5 = (f32[4,72,128]{2,1,0:T(8,128)S(1)}, f32[4,72,128]{2,1,0:T(8,128)S(1)}, u32[]{:S(2)}, u32[]{:S(2)}) collective-permute-start(f32[4,72,128]{2,1,0:T(8,128)S(1)} %get-tuple-element.17.second_ref), channel_id=1, source_target_pairs={{1,2},{3,4},{5,6},{2,1},{4,3},{6,5},{9,10},{11,12},{13,14},{10,9},... | collective-permute-start | bytes 442376 | tf_op jit(solution)/shard_map/ppermute | solution.py:514
  59.5 3.3 %collective-permute-start.4 = (f32[4,72,128]{2,1,0:T(8,128)S(1)}, f32[4,72,128]{2,1,0:T(8,128)S(1)}, u32[]{:S(2)}, u32[]{:S(2)}) collective-permute-start(f32[4,72,128]{2,1,0:T(8,128)S(1)} %get-tuple-element.17.second_ref), channel_id=1, source_target_pairs={{0,1},{2,3},{4,5},{6,7},{1,0},{3,2},{5,4},{7,6},{8,9},{10,11},{12,... | collective-permute-start | bytes 442376 | tf_op jit(solution)/shard_map/ppermute | solution.py:513

commit v6 on v5

--- a/solution.py
+++ b/solution.py
@@ -374,14 +374,15 @@
         def body(step, carry):
             in_turns(
                 *[
-                    moments((step * 2 + side) * tiles_each + k, link_ref, step, parts, k * width)
+                    moments((at * 2 + side) * tiles_each + k, link_ref, at, parts, k * width)
+                    for at in (step * 2, step * 2 + 1)
                     for side, link_ref in enumerate((link_a, link_b))
                     for k in range(tiles_each)
                 ]
             )
             return carry
 
-        lax.fori_loop(0, steps, body, 0)
+        lax.fori_loop(0, steps // 2, body, 0)
 
     @pl.when(wall_ref[0] == 1)
     def _():

time: 76.4 us -> 74.5 us (0.975)
  Pallas kernels: 41.9 us -> 40 us
    pallas_call x1, Pallas kernels: 13.3 us -> 11.4 us  [per_device(): pl.pallas_call(partial(force_kernel, count), out_shape=jax.ShapeDtypeStru...]
where the time goes in v6:
time: 74.5 us; the launch traced here: 74.2 us
  Pallas kernels  40 us (54%)
  starting transfers between devices  26.8 us (36%)
  waiting for transfers between devices  3.01 us (4%)
  other arithmetic  2.57 us (3%)
  local copies, waits for them, and re-layouts  1.05 us (1%)
  between operations  0.77 us (1%)
    pallas_call x1, Pallas kernels, per_device(): pl.pallas_call(partial(flux_kernel, count), out_shape=(pltpu.VMEM((units,...  26.7 us
    pallas_call x1, Pallas kernels, per_device(): pl.pallas_call(partial(force_kernel, count), out_shape=jax.ShapeDtypeStru...  11.4 us
    ppermute x1, starting transfers between devices, per_device(): other = lax.ppermute(other, 'stream', swaps('stream', 1))  10.8 us
    ppermute x1, starting transfers between devices, per_device(): first = lax.ppermute(first, 'stream', swaps('stream', 0))  8.81 us
    ppermute x1, starting transfers between devices, per_device(): mate = lax.ppermute(mid, 'trans', swaps('trans', 0))  3.93 us
    ppermute x1, waiting for transfers between devices, per_device(): other = lax.ppermute(other, 'stream', swaps('stream', 1))  2.13 us
    ppermute x1, starting transfers between devices, per_device(): second_mate = lax.ppermute(second, 'trans', swaps('trans', 0))  1.92 us
    pallas_call x1, Pallas kernels, per_device(): pl.pallas_call(pack_kernel, out_shape=(jax.ShapeDtypeStruct((14, count, l...  1.91 us
  transfers between devices with their start and end apart: 6, of which 3 were waited for; matrix products, arithmetic and copies ran while one was open for 3% of the time, Pallas kernels for 0%

profile of v6, /device:TPU:97, one launch (start us, length us, event | category | flops | bytes accessed | tf_op | source)
XLA Modules:
  0.0 74.2 jit_solution(15129726189707808293)
XLA Ops:
  0.6 1.9 %shard_map.104 = (f32[14,64,128]{2,1,0:T(8,128)}, f32[14,4,128]{2,1,0:T(4,128)}, f32[14,4,128]{2,1,0:T(4,128)}) custom-call(s32[1]{0:T(128)} %bitcast.even_ref, f32[3,64,128]{2,1,0:T(8,128)} %bitcast.25, f32[3,64,128]{2,1,0:T(8,128)} %bitcast.26, f32[4,64,128]{2,1,0:T(8,128)} %bitcast.21, f32[64,128]{1,0:T(8,128)} %bitcast.27, f32[64,128]{1,0:T(8,128)} %bitcast.28, ...), custom_call_target="tpu_custom_call" | custom-call | tf_op jit(solution)/shard_map/pallas_call | solution.py:461
  2.6 8.8 %collective-permute-start = (f32[14,4,128]{2,1,0:T(4,128)}, f32[14,4,128]{2,1,0:T(4,128)S(1)}, u32[]{:S(2)}, u32[]{:S(2)}) collective-permute-start(f32[14,4,128]{2,1,0:T(4,128)} %get-tuple-element.12), channel_id=1, source_target_pairs={{0,8},{16,24},{32,40},{48,56},{64,72},{80,88},{96,104},{112,120},{... | collective-permute-start | bytes 86024 | tf_op jit(solution)/shard_map/ppermute | solution.py:480
  11.4 10.8 %collective-permute-start.1 = (f32[14,4,128]{2,1,0:T(4,128)}, f32[14,4,128]{2,1,0:T(4,128)S(1)}, u32[]{:S(2)}, u32[]{:S(2)}) collective-permute-start(f32[14,4,128]{2,1,0:T(4,128)} %get-tuple-element.13), channel_id=1, source_target_pairs={{8,16},{24,32},{40,48},{56,64},{72,80},{88,96},{104,112},{120,128}... | collective-permute-start | bytes 86024 | tf_op jit(solution)/shard_map/ppermute | solution.py:481
  22.2 0.7 convert_element_type.14
  22.8 0.0 collective-permute-done
  22.8 2.1 %collective-permute-done.1 = f32[14,4,128]{2,1,0:T(4,128)S(1)} collective-permute-done((f32[14,4,128]{2,1,0:T(4,128)}, f32[14,4,128]{2,1,0:T(4,128)S(1)}, u32[]{:S(2)}, u32[]{:S(2)}) %collective-permute-start.1) | collective-permute-done | bytes 28704 | tf_op jit(solution)/shard_map/ppermute | solution.py:481
  25.0 1.1 %pad_maximum_fusion.ext_ref = f32[14,72,128]{2,1,0:T(8,128)S(1)} fusion(f32[14,4,128]{2,1,0:T(4,128)S(1)} %bitcast.23, f32[14,4,128]{2,1,0:T(4,128)S(1)} %bitcast.22, f32[14,64,128]{2,1,0:T(8,128)} %get-tuple-element.11), kind=kLoop, calls=%fused_computation | loop fusion | flops 258048 | bytes 1032192 | tf_op jit(solution)/shard_map/concatenate | solution.py:484
  26.1 3.9 %collective-permute-start.2 = (f32[9,72,128]{2,1,0:T(8,128)S(1)}, f32[9,72,128]{2,1,0:T(8,128)S(1)}, u32[]{:S(2)}, u32[]{:S(2)}) collective-permute-start(f32[9,72,128]{2,1,0:T(8,128)S(1)} %slice.13), channel_id=1, source_target_pairs={{0,1},{2,3},{4,5},{6,7},{1,0},{3,2},{5,4},{7,6},{8,9},{10,11},{12,... | collective-permute-start | bytes 995336 | tf_op jit(solution)/shard_map/ppermute | solution.py:486
  30.0 0.1 add.53
  30.1 0.1 add.54
  30.2 0.1 pad_add_fusion.wall_ref
  30.3 0.7 pad_maximum_fusion.1.param_ref
  31.0 0.2 collective-permute-done.2.mate_ref
  31.2 0.7 collective-permute-start.3
  31.9 0.1 convert_element_type.13
  32.1 0.0 collective-permute-done.3.next_ref
  32.1 26.7 %shard_map.105 = (bf16[34,128,1152]{2,1,0:T(8,128)(2,1)S(1)}, bf16[34,128,1152]{2,1,0:T(8,128)(2,1)S(1)}, f32[4,72,128]{2,1,0:T(8,128)S(1)}, f32[4,72,128]{2,1,0:T(8,128)S(1)}) custom-call(s32[648]{0:T(1024)S(1)} %fusion.3.codes_ref, s32[2]{0:T(128)S(1)} %pad_add_fusion.wall_ref, f32[8]{0:T(128)S(1)} %pad_maximum_fusion.1.param_ref, ...), custom_call_target="tpu_custom_call" | custom-call | tf_op jit(solution)/shard_map/pallas_call | solution.py:491
  58.8 0.7 collective-permute-start.5
  59.5 1.9 %collective-permute-start.4 = (f32[4,72,128]{2,1,0:T(8,128)S(1)}, f32[4,72,128]{2,1,0:T(8,128)S(1)}, u32[]{:S(2)}, u32[]{:S(2)}) collective-permute-start(f32[4,72,128]{2,1,0:T(8,128)S(1)} %get-tuple-element.17.second_ref), channel_id=1, source_target_pairs={{0,1},{2,3},{4,5},{6,7},{1,0},{3,2},{5,4},{7,6},{8,9},{10,11},{12,... | collective-permute-start | bytes 442376 | tf_op jit(solution)/shard_map/ppermute | solution.py:514
  61.4 0.7 slice_bitcast_fusion
  62.1 0.0 collective-permute-done.5.second_next_ref
  62.1 0.7 collective-permute-done.4.second_mate_ref
  62.8 11.4 %shard_map.106 = f32[3,64,128]{2,1,0:T(8,128)} custom-call(s32[648]{0:T(1024)S(1)} %fusion.3.codes_ref, s32[2]{0:T(128)S(1)} %pad_add_fusion.wall_ref, f32[14,72,128]{2,1,0:T(8,128)S(1)} %pad_maximum_fusion.ext_ref, f32[9,72,128]{2,1,0:T(8,128)S(1)} %collective-permute-done.2.mate_ref, f32[9,72,128]{2,1,0:T(8,128)S(1)} %collective-permute-done.3.next_ref, ...), custom_call_target="tpu_custom_call" | custom-call | tf_op jit(solution)/shard_map/pallas_call | solution.py:516
  (5 shorter events, 0.1 us)
Async XLA Ops:
  2.6 20.3 %collective-permute-start = (f32[14,4,128]{2,1,0:T(4,128)}, f32[14,4,128]{2,1,0:T(4,128)S(1)}, u32[]{:S(2)}, u32[]{:S(2)}) collective-permute-start(f32[14,4,128]{2,1,0:T(4,128)} %get-tuple-element.12), channel_id=1, source_target_pairs={{0,8},{16,24},{32,40},{48,56},{64,72},{80,88},{96,104},{112,120},{... | collective-permute-start | bytes 86024 | tf_op jit(solution)/shard_map/ppermute | solution.py:480
  11.4 13.6 %collective-permute-start.1 = (f32[14,4,128]{2,1,0:T(4,128)}, f32[14,4,128]{2,1,0:T(4,128)S(1)}, u32[]{:S(2)}, u32[]{:S(2)}) collective-permute-start(f32[14,4,128]{2,1,0:T(4,128)} %get-tuple-element.13), channel_id=1, source_target_pairs={{8,16},{24,32},{40,48},{56,64},{72,80},{88,96},{104,112},{120,128}... | collective-permute-start | bytes 86024 | tf_op jit(solution)/shard_map/ppermute | solution.py:481
  26.1 5.2 %collective-permute-start.2 = (f32[9,72,128]{2,1,0:T(8,128)S(1)}, f32[9,72,128]{2,1,0:T(8,128)S(1)}, u32[]{:S(2)}, u32[]{:S(2)}) collective-permute-start(f32[9,72,128]{2,1,0:T(8,128)S(1)} %slice.13), channel_id=1, source_target_pairs={{0,1},{2,3},{4,5},{6,7},{1,0},{3,2},{5,4},{7,6},{8,9},{10,11},{12,... | collective-permute-start | bytes 995336 | tf_op jit(solution)/shard_map/ppermute | solution.py:486
  31.2 0.9 %collective-permute-start.3 = (f32[9,72,128]{2,1,0:T(8,128)S(1)}, f32[9,72,128]{2,1,0:T(8,128)S(1)}, u32[]{:S(2)}, u32[]{:S(2)}) collective-permute-start(f32[9,72,128]{2,1,0:T(8,128)S(1)} %slice.13), channel_id=1, source_target_pairs={{1,2},{3,4},{5,6},{2,1},{4,3},{6,5},{9,10},{11,12},{13,14},{10,9},... | collective-permute-start | bytes 995336 | tf_op jit(solution)/shard_map/ppermute | solution.py:488
  58.8 3.3 %collective-permute-start.5 = (f32[4,72,128]{2,1,0:T(8,128)S(1)}, f32[4,72,128]{2,1,0:T(8,128)S(1)}, u32[]{:S(2)}, u32[]{:S(2)}) collective-permute-start(f32[4,72,128]{2,1,0:T(8,128)S(1)} %get-tuple-element.17.second_ref), channel_id=1, source_target_pairs={{1,2},{3,4},{5,6},{2,1},{4,3},{6,5},{9,10},{11,12},{13,14},{10,9},... | collective-permute-start | bytes 442376 | tf_op jit(solution)/shard_map/ppermute | solution.py:515
  59.5 3.3 %collective-permute-start.4 = (f32[4,72,128]{2,1,0:T(8,128)S(1)}, f32[4,72,128]{2,1,0:T(8,128)S(1)}, u32[]{:S(2)}, u32[]{:S(2)}) collective-permute-start(f32[4,72,128]{2,1,0:T(8,128)S(1)} %get-tuple-element.17.second_ref), channel_id=1, source_target_pairs={{0,1},{2,3},{4,5},{6,7},{1,0},{3,2},{5,4},{7,6},{8,9},{10,11},{12,... | collective-permute-start | bytes 442376 | tf_op jit(solution)/shard_map/ppermute | solution.py:514

commit v7 on v6

--- a/solution.py
+++ b/solution.py
@@ -375,14 +375,14 @@
             in_turns(
                 *[
                     moments((at * 2 + side) * tiles_each + k, link_ref, at, parts, k * width)
-                    for at in (step * 2, step * 2 + 1)
+                    for at in (step * 4, step * 4 + 1, step * 4 + 2, step * 4 + 3)
                     for side, link_ref in enumerate((link_a, link_b))
                     for k in range(tiles_each)
                 ]
             )
             return carry
 
-        lax.fori_loop(0, steps // 2, body, 0)
+        lax.fori_loop(0, steps // 4, body, 0)
 
     @pl.when(wall_ref[0] == 1)
     def _():

time: 74.5 us -> 73.6 us (0.988)
  Pallas kernels: 40 us -> 39.1 us
    pallas_call x1, Pallas kernels: 11.4 us -> 10.5 us  [per_device(): pl.pallas_call(partial(force_kernel, count), out_shape=jax.ShapeDtypeStru...]
where the time goes in v7:
time: 73.6 us; the launch traced here: 73.3 us
  Pallas kernels  39.1 us (53%)
  starting transfers between devices  26.8 us (36%)
  waiting for transfers between devices  3.01 us (4%)
  other arithmetic  2.57 us (3%)
  local copies, waits for them, and re-layouts  1.05 us (1%)
  between operations  0.77 us (1%)
    pallas_call x1, Pallas kernels, per_device(): pl.pallas_call(partial(flux_kernel, count), out_shape=(pltpu.VMEM((units,...  26.7 us
    ppermute x1, starting transfers between devices, per_device(): other = lax.ppermute(other, 'stream', swaps('stream', 1))  10.8 us
    pallas_call x1, Pallas kernels, per_device(): pl.pallas_call(partial(force_kernel, count), out_shape=jax.ShapeDtypeStru...  10.5 us
    ppermute x1, starting transfers between devices, per_device(): first = lax.ppermute(first, 'stream', swaps('stream', 0))  8.81 us
    ppermute x1, starting transfers between devices, per_device(): mate = lax.ppermute(mid, 'trans', swaps('trans', 0))  3.93 us
    ppermute x1, waiting for transfers between devices, per_device(): other = lax.ppermute(other, 'stream', swaps('stream', 1))  2.13 us
    ppermute x1, starting transfers between devices, per_device(): second_mate = lax.ppermute(second, 'trans', swaps('trans', 0))  1.92 us
    pallas_call x1, Pallas kernels, per_device(): pl.pallas_call(pack_kernel, out_shape=(jax.ShapeDtypeStruct((14, count, l...  1.91 us
  transfers between devices with their start and end apart: 6, of which 3 were waited for; matrix products, arithmetic and copies ran while one was open for 3% of the time, Pallas kernels for 0%

profile of v7, /device:TPU:97, one launch (start us, length us, event | category | flops | bytes accessed | tf_op | source)
XLA Modules:
  0.0 73.3 jit_solution(12598350147731221158)
XLA Ops:
  0.6 1.9 %shard_map.104 = (f32[14,64,128]{2,1,0:T(8,128)}, f32[14,4,128]{2,1,0:T(4,128)}, f32[14,4,128]{2,1,0:T(4,128)}) custom-call(s32[1]{0:T(128)} %bitcast.even_ref, f32[3,64,128]{2,1,0:T(8,128)} %bitcast.25, f32[3,64,128]{2,1,0:T(8,128)} %bitcast.26, f32[4,64,128]{2,1,0:T(8,128)} %bitcast.21, f32[64,128]{1,0:T(8,128)} %bitcast.27, f32[64,128]{1,0:T(8,128)} %bitcast.28, ...), custom_call_target="tpu_custom_call" | custom-call | tf_op jit(solution)/shard_map/pallas_call | solution.py:461
  2.6 8.8 %collective-permute-start = (f32[14,4,128]{2,1,0:T(4,128)}, f32[14,4,128]{2,1,0:T(4,128)S(1)}, u32[]{:S(2)}, u32[]{:S(2)}) collective-permute-start(f32[14,4,128]{2,1,0:T(4,128)} %get-tuple-element.12), channel_id=1, source_target_pairs={{0,8},{16,24},{32,40},{48,56},{64,72},{80,88},{96,104},{112,120},{... | collective-permute-start | bytes 86024 | tf_op jit(solution)/shard_map/ppermute | solution.py:480
  11.4 10.8 %collective-permute-start.1 = (f32[14,4,128]{2,1,0:T(4,128)}, f32[14,4,128]{2,1,0:T(4,128)S(1)}, u32[]{:S(2)}, u32[]{:S(2)}) collective-permute-start(f32[14,4,128]{2,1,0:T(4,128)} %get-tuple-element.13), channel_id=1, source_target_pairs={{8,16},{24,32},{40,48},{56,64},{72,80},{88,96},{104,112},{120,128}... | collective-permute-start | bytes 86024 | tf_op jit(solution)/shard_map/ppermute | solution.py:481
  22.2 0.7 convert_element_type.14
  22.8 0.0 collective-permute-done
  22.8 2.1 %collective-permute-done.1 = f32[14,4,128]{2,1,0:T(4,128)S(1)} collective-permute-done((f32[14,4,128]{2,1,0:T(4,128)}, f32[14,4,128]{2,1,0:T(4,128)S(1)}, u32[]{:S(2)}, u32[]{:S(2)}) %collective-permute-start.1) | collective-permute-done | bytes 28704 | tf_op jit(solution)/shard_map/ppermute | solution.py:481
  25.0 1.1 %pad_maximum_fusion.ext_ref = f32[14,72,128]{2,1,0:T(8,128)S(1)} fusion(f32[14,4,128]{2,1,0:T(4,128)S(1)} %bitcast.23, f32[14,4,128]{2,1,0:T(4,128)S(1)} %bitcast.22, f32[14,64,128]{2,1,0:T(8,128)} %get-tuple-element.11), kind=kLoop, calls=%fused_computation | loop fusion | flops 258048 | bytes 1032192 | tf_op jit(solution)/shard_map/concatenate | solution.py:484
  26.1 3.9 %collective-permute-start.2 = (f32[9,72,128]{2,1,0:T(8,128)S(1)}, f32[9,72,128]{2,1,0:T(8,128)S(1)}, u32[]{:S(2)}, u32[]{:S(2)}) collective-permute-start(f32[9,72,128]{2,1,0:T(8,128)S(1)} %slice.13), channel_id=1, source_target_pairs={{0,1},{2,3},{4,5},{6,7},{1,0},{3,2},{5,4},{7,6},{8,9},{10,11},{12,... | collective-permute-start | bytes 995336 | tf_op jit(solution)/shard_map/ppermute | solution.py:486
  30.0 0.1 add.53
  30.1 0.1 add.54
  30.2 0.1 pad_add_fusion.wall_ref
  30.3 0.7 pad_maximum_fusion.1.param_ref
  31.0 0.2 collective-permute-done.2.mate_ref
  31.2 0.7 collective-permute-start.3
  31.9 0.1 convert_element_type.13
  32.1 0.0 collective-permute-done.3.next_ref
  32.1 26.7 %shard_map.105 = (bf16[34,128,1152]{2,1,0:T(8,128)(2,1)S(1)}, bf16[34,128,1152]{2,1,0:T(8,128)(2,1)S(1)}, f32[4,72,128]{2,1,0:T(8,128)S(1)}, f32[4,72,128]{2,1,0:T(8,128)S(1)}) custom-call(s32[648]{0:T(1024)S(1)} %fusion.3.codes_ref, s32[2]{0:T(128)S(1)} %pad_add_fusion.wall_ref, f32[8]{0:T(128)S(1)} %pad_maximum_fusion.1.param_ref, ...), custom_call_target="tpu_custom_call" | custom-call | tf_op jit(solution)/shard_map/pallas_call | solution.py:491
  58.8 0.7 collective-permute-start.5
  59.5 1.9 %collective-permute-start.4 = (f32[4,72,128]{2,1,0:T(8,128)S(1)}, f32[4,72,128]{2,1,0:T(8,128)S(1)}, u32[]{:S(2)}, u32[]{:S(2)}) collective-permute-start(f32[4,72,128]{2,1,0:T(8,128)S(1)} %get-tuple-element.17.second_ref), channel_id=1, source_target_pairs={{0,1},{2,3},{4,5},{6,7},{1,0},{3,2},{5,4},{7,6},{8,9},{10,11},{12,... | collective-permute-start | bytes 442376 | tf_op jit(solution)/shard_map/ppermute | solution.py:514
  61.5 0.7 slice_bitcast_fusion
  62.1 0.0 collective-permute-done.5.second_next_ref
  62.1 0.7 collective-permute-done.4.second_mate_ref
  62.8 10.5 %shard_map.106 = f32[3,64,128]{2,1,0:T(8,128)} custom-call(s32[648]{0:T(1024)S(1)} %fusion.3.codes_ref, s32[2]{0:T(128)S(1)} %pad_add_fusion.wall_ref, f32[14,72,128]{2,1,0:T(8,128)S(1)} %pad_maximum_fusion.ext_ref, f32[9,72,128]{2,1,0:T(8,128)S(1)} %collective-permute-done.2.mate_ref, f32[9,72,128]{2,1,0:T(8,128)S(1)} %collective-permute-done.3.next_ref, ...), custom_call_target="tpu_custom_call" | custom-call | tf_op jit(solution)/shard_map/pallas_call | solution.py:516
  (5 shorter events, 0.1 us)
Async XLA Ops:
  2.6 20.3 %collective-permute-start = (f32[14,4,128]{2,1,0:T(4,128)}, f32[14,4,128]{2,1,0:T(4,128)S(1)}, u32[]{:S(2)}, u32[]{:S(2)}) collective-permute-start(f32[14,4,128]{2,1,0:T(4,128)} %get-tuple-element.12), channel_id=1, source_target_pairs={{0,8},{16,24},{32,40},{48,56},{64,72},{80,88},{96,104},{112,120},{... | collective-permute-start | bytes 86024 | tf_op jit(solution)/shard_map/ppermute | solution.py:480
  11.4 13.6 %collective-permute-start.1 = (f32[14,4,128]{2,1,0:T(4,128)}, f32[14,4,128]{2,1,0:T(4,128)S(1)}, u32[]{:S(2)}, u32[]{:S(2)}) collective-permute-start(f32[14,4,128]{2,1,0:T(4,128)} %get-tuple-element.13), channel_id=1, source_target_pairs={{8,16},{24,32},{40,48},{56,64},{72,80},{88,96},{104,112},{120,128}... | collective-permute-start | bytes 86024 | tf_op jit(solution)/shard_map/ppermute | solution.py:481
  26.1 5.2 %collective-permute-start.2 = (f32[9,72,128]{2,1,0:T(8,128)S(1)}, f32[9,72,128]{2,1,0:T(8,128)S(1)}, u32[]{:S(2)}, u32[]{:S(2)}) collective-permute-start(f32[9,72,128]{2,1,0:T(8,128)S(1)} %slice.13), channel_id=1, source_target_pairs={{0,1},{2,3},{4,5},{6,7},{1,0},{3,2},{5,4},{7,6},{8,9},{10,11},{12,... | collective-permute-start | bytes 995336 | tf_op jit(solution)/shard_map/ppermute | solution.py:486
  31.2 0.9 %collective-permute-start.3 = (f32[9,72,128]{2,1,0:T(8,128)S(1)}, f32[9,72,128]{2,1,0:T(8,128)S(1)}, u32[]{:S(2)}, u32[]{:S(2)}) collective-permute-start(f32[9,72,128]{2,1,0:T(8,128)S(1)} %slice.13), channel_id=1, source_target_pairs={{1,2},{3,4},{5,6},{2,1},{4,3},{6,5},{9,10},{11,12},{13,14},{10,9},... | collective-permute-start | bytes 995336 | tf_op jit(solution)/shard_map/ppermute | solution.py:488
  58.8 3.3 %collective-permute-start.5 = (f32[4,72,128]{2,1,0:T(8,128)S(1)}, f32[4,72,128]{2,1,0:T(8,128)S(1)}, u32[]{:S(2)}, u32[]{:S(2)}) collective-permute-start(f32[4,72,128]{2,1,0:T(8,128)S(1)} %get-tuple-element.17.second_ref), channel_id=1, source_target_pairs={{1,2},{3,4},{5,6},{2,1},{4,3},{6,5},{9,10},{11,12},{13,14},{10,9},... | collective-permute-start | bytes 442376 | tf_op jit(solution)/shard_map/ppermute | solution.py:515
  59.5 3.3 %collective-permute-start.4 = (f32[4,72,128]{2,1,0:T(8,128)S(1)}, f32[4,72,128]{2,1,0:T(8,128)S(1)}, u32[]{:S(2)}, u32[]{:S(2)}) collective-permute-start(f32[4,72,128]{2,1,0:T(8,128)S(1)} %get-tuple-element.17.second_ref), channel_id=1, source_target_pairs={{0,1},{2,3},{4,5},{6,7},{1,0},{3,2},{5,4},{7,6},{8,9},{10,11},{12,... | collective-permute-start | bytes 442376 | tf_op jit(solution)/shard_map/ppermute | solution.py:514
